TPU v7x, 32 devices: a whole 2x2x4 slice. The times are simulated.
32 devices in a mesh: grp: 2 (over y), path: 16 (over z, x, core).
Axes of the slice: x: 2, y: 2, z: 4, core: 2. Of those that a mesh axis runs over, the one named last changes fastest.
Arguments:
- start_state: float32 [100, 4096], P(None, 'path'), may hold values from -6 to 6
- shocks: float32 [100, 4096], P(None, 'path'), may hold values from -6 to 6
- drift_rate: float32 [100], replicated, may hold values from -0.5 to 0.5
- vol_curve: float32 [100], replicated, may hold values from 0.2 to 1
- weight_in: float32 [2, 1024, 100], P('grp'), may hold values from -0.625 to 0.625
- bias_in: float32 [2, 1024], P('grp'), may hold values from -3 to 3
- weight_out: float32 [2, 1024], P('grp'), may hold values from -0.1875 to 0.1875
- default_date: int32 [4096], P('path'), may hold values from 1 to 3
- netting_set: int32 [4096], P('path'), may hold values from 0 to 15
- loss_given: float32 [16], replicated, may hold values from 0.3 to 0.9
Outputs:
- residual: float32 [2, 4096], P('grp', 'path')
- step_weight_in: float32 [2, 1024, 100], P('grp')
- step_bias: float32 [2, 1024], P('grp')
- step_weight_out: float32 [2, 1024], P('grp')
- curve_step: float32 [2, 100], replicated
All inputs are finite; a program needn't handle non-finite values.
Results may differ from a plain program's by a relative error of at most 0.0003.
Values sent between devices are 32-bit elements; how exact they have to be, the bound alone decides.
A program may use at most 64 MiB of HBM per device.

v0:
```python
import jax
import jax.numpy as jnp
from jax import lax
from jax.sharding import PartitionSpec as P

step_dt = 0.25
root_dt = 0.5
growth_factor = 1.0075
fund_spread = 0.5
norm_eps = 1e-06


def from_behind(shard, axis, by):
    devices = lax.axis_size(axis)
    pairs = [(i, i + by) for i in range(devices) if 0 <= i + by < devices]
    return lax.ppermute(shard, axis, pairs)


def net_parts(weight, bias, outer, start_state, shocks, drift_rate, vol_curve):
    hp = lax.Precision.HIGHEST
    next_state = start_state + drift_rate[:, None] * step_dt + vol_curve[:, None] * root_dt * shocks
    hidden_now = jnp.tanh(jnp.dot(weight, start_state, precision=hp) + bias[:, None])
    hidden_next = jnp.tanh(jnp.dot(weight, next_state, precision=hp) + bias[:, None])
    value_now = jnp.dot(outer, hidden_now, precision=hp)
    value_next = jnp.dot(outer, hidden_next, precision=hp)
    slope = outer[:, None] * (1.0 - hidden_now * hidden_now)
    delta = vol_curve[:, None] * jnp.dot(weight.T, slope, precision=hp)
    return (value_now, value_next, delta)


def set_losses(netting_set, loss_given):
    sets = jnp.arange(loss_given.shape[0], dtype=jnp.int32)
    return jnp.sum(
        jnp.where(netting_set[None, :] == sets[:, None], loss_given[:, None], jnp.float32(0.0)),
        axis=0,
    )


def body(
    start_state,
    shocks,
    drift_rate,
    vol_curve,
    weight_in,
    bias_in,
    weight_out,
    default_date,
    netting_set,
    loss_given,
):
    grp_index = lax.axis_index("grp")
    clean_side = grp_index == 0
    total = start_state.shape[1] * lax.axis_size("path")

    def parts_fn(weight, bias, outer, drift, vol):
        return net_parts(weight, bias, outer, start_state, shocks, drift, vol)

    parts_fn = jax.checkpoint(parts_fn)
    (value_now, value_next, delta), pullback = jax.vjp(
        parts_fn, weight_in[0], bias_in[0], weight_out[0], drift_rate, vol_curve
    )
    packed = jnp.concatenate([value_next[None, :], delta], axis=0)
    received = from_behind(packed, "grp", 1)
    other_next = received[0]
    other_delta = received[1:]
    drift_term = root_dt * jnp.sum(delta * shocks, axis=0)
    res_clean = value_next - growth_factor * value_now - drift_term
    loss_row = set_losses(netting_set, loss_given)
    margin = jnp.sqrt(jnp.sum(other_delta * other_delta, axis=0) + norm_eps)
    defaulted = default_date == 1
    target = jnp.where(defaulted, loss_row * jax.nn.softplus(other_next), value_next)
    res_xva = target - growth_factor * value_now - drift_term + step_dt * fund_spread * margin
    residual = jnp.where(clean_side, res_clean, res_xva)
    weighted = residual / jnp.float32(total)
    keep_next = jnp.where(
        clean_side, jnp.float32(1.0), jnp.where(defaulted, jnp.float32(0.0), jnp.float32(1.0))
    )
    cot_now = -growth_factor * weighted
    cot_next = weighted * keep_next
    cot_delta = -root_dt * weighted[None, :] * shocks
    xva_only = jnp.where(clean_side, jnp.float32(0.0), jnp.float32(1.0))
    send_next = (
        xva_only
        * weighted
        * jnp.where(defaulted, loss_row * jax.nn.sigmoid(other_next), jnp.float32(0.0))
    )
    send_delta = xva_only * (weighted * step_dt * fund_spread / margin)[None, :] * other_delta
    send_packed = jnp.concatenate([send_next[None, :], send_delta], axis=0)
    back_packed = from_behind(send_packed, "grp", -1)
    back_next = back_packed[0]
    back_delta = back_packed[1:]
    grad_w, grad_b, grad_o, grad_drift, grad_vol = pullback(
        (cot_now, cot_next + back_next, cot_delta + back_delta)
    )
    sum_drift, sum_vol = lax.psum((grad_drift, grad_vol), ("grp", "path"))
    curve = jnp.stack([sum_drift, sum_vol])
    curve_step = curve / jnp.sqrt(jnp.mean(curve * curve) + norm_eps)
    count_w = grad_w.shape[0] * grad_w.shape[1] + 2 * grad_w.shape[0]
    sum_w, sum_b, sum_o = lax.psum((grad_w, grad_b, grad_o), "path")
    sumsq = jnp.sum(sum_w * sum_w) + jnp.sum(sum_b * sum_b) + jnp.sum(sum_o * sum_o)
    scale = jnp.sqrt(sumsq / count_w + norm_eps)
    step_w, step_b, step_o = (sum_w / scale, sum_b / scale, sum_o / scale)
    return (residual[None, :], step_w[None], step_b[None], step_o[None], curve_step)


def solution(mesh):
    return jax.shard_map(
        body,
        mesh=mesh,
        in_specs=(
            P(None, "path"),
            P(None, "path"),
            P(),
            P(),
            P("grp", None, None),
            P("grp", None),
            P("grp", None),
            P("path"),
            P("path"),
            P(),
        ),
        out_specs=(P("grp", "path"), P("grp", None, None), P("grp", None), P("grp", None), P()),
        check_vma=False,
    )
```

profile of v0, /device:TPU:0, one launch (start us, length us, event | category | flops | bytes accessed | tf_op | source)
XLA Modules:
  0.0 186.5 jit_solution(7654300226741225782)
XLA Ops:
  7.2 0.7 broadcast_multiply_fusion.3
  7.9 2.2 %fusion.2 = f32[1024,256]{1,0:T(8,128)S(1)} fusion(f32[100,256]{1,0:T(8,128)} %param.10, f32[1024]{0:T(1024)} %bitcast.64, f32[1,1024,100]{1,0,2:T(1,128)} %param.14), kind=kOutput, calls=%fused_computation.5 | convolution fusion | flops 314834944 | bytes 1564672 | tf_op jit(solution)/shard_map/jvp()/dot_general | solution.py:22
  10.2 1.1 fusion.4
  11.3 0.9 fusion.32
  12.9 0.9 multiply_reduce_fusion.4
  13.8 4.9 %collective-permute-start = (f32[101,256]{1,0:T(8,128)S(1)}, f32[101,256]{1,0:T(8,128)S(1)}, u32[]{:S(2)}, u32[]{:S(2)}) collective-permute-start(f32[101,256]{1,0:T(8,128)S(1)} %pad_maximum_fusion), channel_id=1, source_target_pairs={{0,16},{1,17},{2,18},{3,19},{4,20},{5,21},{6,22},{7,23},{8,24},{9,... | collective-permute-start | bytes 310280 | tf_op jit(solution)/shard_map/ppermute | solution.py:16
  20.1 0.9 collective-permute-done
  21.8 1.5 collective-permute-start.1
  23.3 5.0 %collective-permute-done.1 = f32[101,256]{1,0:T(8,128)S(1)} collective-permute-done((f32[101,256]{1,0:T(8,128)S(1)}, f32[101,256]{1,0:T(8,128)S(1)}, u32[]{:S(2)}, u32[]{:S(2)}) %collective-permute-start.1) | collective-permute-done | bytes 103456 | tf_op jit(solution)/shard_map/ppermute | solution.py:16
  28.4 1.1 fusion.1
  29.5 0.9 fusion.6
  30.5 1.3 fusion.12
  31.8 1.1 fusion
  32.9 0.9 fusion.47
  33.9 2.6 %multiply_reduce_fusion = (f32[1024]{0:T(1024)S(1)}, f32[1024]{0:T(1024)S(1)}, f32[1024]{0:T(1024)S(1)}, f32[1024,256]{1,0:T(8,128)}) fusion(f32[1024,256]{1,0:T(8,128)S(1)} %fusion.1, f32[256]{0:T(256)S(1)} %get-tuple-element.24, f32[1024]{0:T(1024)S(1)} %bitcast.61, f32[1024,256]{1,0:T(8,128)S(1)} %fusion, f32[256]{0:T(256)S(1)} %get-tuple-element.21, ...), kind=kOutput, calls=%fused_computation.17 | convolution fusion | flops 320100352 | bytes 3676560 | tf_op jit(solution)/shard_map/transpose(jvp(jvp()))/checkpoint/dot_general | solution.py:27
  36.4 1.0 fusion.49
  37.4 1.4 convolution_add_fusion.5
  38.8 39.6 %all-reduce = (f32[1,100]{1,0:T(1,128)S(1)}, f32[1,100]{1,0:T(1,128)S(1)}) all-reduce(f32[1,100]{1,0:T(1,128)S(1)} %add_bitcast_fusion, f32[1,100]{1,0:T(1,128)S(1)} %multiply_bitcast_fusion), channel_id=1, replica_groups=mesh['grp'=2,'path'=16] {'grp','path'}, use_global_device_ids=true, to_apply=%region_16.17 | all-reduce | flops 200 | bytes 1600 | tf_op jit(solution)/shard_map/psum | solution.py:95
  79.7 1.0 fusion.48
  80.9 2.3 %convolution_add_fusion.4 = f32[1024,100]{0,1:T(8,128)} fusion(f32[1024,100]{0,1:T(8,128)S(1)} %convolution_add_fusion.5, f32[100,256]{1,0:T(8,128)S(1)} %copy-done.1, f32[1024,256]{1,0:T(8,128)S(1)} %fusion.1, f32[1024,256]{1,0:T(8,128)S(1)} %copy-done.4, f32[256]{0:T(256)S(1)} %get-tuple-element.24, f32[1024]{0:T(1024)S(1)} %bitcast.63), kind=kOutput, calls=%fused_computation.9 | convolution fusion | flops 317296640 | bytes 3023872 | tf_op jit(solution)/shard_map/transpose(jvp(jvp()))/checkpoint/dot_general | solution.py:22
  83.3 32.6 %all-reduce.1 = (f32[1024]{0:T(1024)S(1)}, f32[1024]{0:T(1024)S(1)}) all-reduce(f32[1024]{0:T(1024)S(1)} %add_any.28, f32[1024]{0:T(1024)S(1)} %add_add_fusion), channel_id=1, replica_groups=mesh['grp'=2,'path'=16] {'path'}, use_global_device_ids=true, to_apply=%region_7.8 | all-reduce | flops 2048 | bytes 16384 | tf_op jit(solution)/shard_map/psum | solution.py:99
  117.6 55.9 %all-reduce.4.cloned.1.call-done = f32[1024,100]{0,1:T(8,128)} async-done(((f32[1024,100]{0,1:T(8,128)}), f32[1024,100]{0,1:T(8,128)}) %all-reduce.4.cloned.1.call-update) | async-done | bytes 409616 | tf_op jit(solution)/shard_map/psum | solution.py:99
  173.5 1.8 multiply_reduce_fusion.1
  178.5 1.2 copy.24
  (54 shorter events, 6.9 us)
Async XLA Ops:
  7.2 166.3 %all-reduce.4.cloned.1.call-start = ((), (), s32[]{:S(2)}) async-start(), calls=%async_computation | async-start | bytes 851968 | tf_op jit(solution)/shard_map/psum | solution.py:99
  7.9 2.2 %copy-start = (f32[1,1024,100]{1,0,2:T(1,128)S(1)}, f32[1,1024,100]{1,0,2:T(1,128)}, u32[]{:S(2)}) copy-start(f32[1,1024,100]{1,0,2:T(1,128)} %param.14) | copy-start | bytes 1228804
  7.9 2.2 %copy-start.1 = (f32[100,256]{1,0:T(8,128)S(1)}, f32[100,256]{1,0:T(8,128)}, u32[]{:S(2)}) copy-start(f32[100,256]{1,0:T(8,128)} %param.10) | copy-start | bytes 307204
  7.9 2.2 %copy-start.2 = (f32[100,256]{1,0:T(8,128)S(1)}, f32[100,256]{1,0:T(8,128)}, u32[]{:S(2)}) copy-start(f32[100,256]{1,0:T(8,128)} %param.11) | copy-start | bytes 307204
  7.9 2.3 %copy-start.6 = (f32[1,1024]{1,0:T(1,128)S(1)}, f32[1,1024]{1,0:T(1,128)}, u32[]{:S(2)}) copy-start(f32[1,1024]{1,0:T(1,128)} %param.15) | copy-start | bytes 12292
  10.2 1.2 copy-start.5
  12.2 0.7 copy-start.9
  13.8 7.2 %collective-permute-start = (f32[101,256]{1,0:T(8,128)S(1)}, f32[101,256]{1,0:T(8,128)S(1)}, u32[]{:S(2)}, u32[]{:S(2)}) collective-permute-start(f32[101,256]{1,0:T(8,128)S(1)} %pad_maximum_fusion), channel_id=1, source_target_pairs={{0,16},{1,17},{2,18},{3,19},{4,20},{5,21},{6,22},{7,23},{8,24},{9,... | collective-permute-start | bytes 310280 | tf_op jit(solution)/shard_map/ppermute | solution.py:16
  19.3 0.7 copy-start.10
  19.3 0.7 copy-start.11
  21.0 0.7 copy-start.7
  21.7 6.7 %copy-start.8 = (f32[256]{0:T(256)}, f32[256]{0:T(256)S(1)}, u32[]{:S(2)}) copy-start(f32[256]{0:T(256)S(1)} %get-tuple-element.45) | copy-start | bytes 3076
  21.8 6.6 %collective-permute-start.1 = (f32[101,256]{1,0:T(8,128)S(1)}, f32[101,256]{1,0:T(8,128)S(1)}, u32[]{:S(2)}, u32[]{:S(2)}) collective-permute-start(f32[101,256]{1,0:T(8,128)S(1)} %pad_maximum_fusion.1), channel_id=1, source_target_pairs={{16,0},{17,1},{18,2},{19,3},{20,4},{21,5},{22,6},{23,7},{24,8},{25... | collective-permute-start | bytes 310280 | tf_op jit(solution)/shard_map/ppermute | solution.py:16
  30.4 1.3 copy-start.12
  79.7 1.2 copy-start.4
  173.5 5.0 %copy-start.3 = (f32[1024,100]{0,1:T(8,128)S(1)}, f32[1024,100]{0,1:T(8,128)}, u32[]{:S(2)}) copy-start(f32[1024,100]{0,1:T(8,128)} %all-reduce.4.cloned.1.call-done) | copy-start | bytes 1228804
Sparse Core Ops, SparseCore 0:
  83.3 90.0 all-reduce.3
where the time goes:
time: 187 us
  blocking collectives  72.2 us (39%)
  waiting for transfers between devices  61.8 us (33%)
  matrix products  19.3 us (10%)
  between operations  17 us (9%)
  starting transfers between devices  6.39 us (3%)
  other arithmetic  6.35 us (3%)
  local copies, waits for them, and re-layouts  3.58 us (2%)
    psum x1, waiting for transfers between devices, body(): sum_w, sum_b, sum_o = lax.psum((grad_w, grad_b, grad_o), 'path')  55.9 us
    psum x1, blocking collectives, body(): sum_drift, sum_vol = lax.psum((grad_drift, grad_vol), ('grp', 'path'))  39.6 us
    psum x1, blocking collectives, body(): sum_w, sum_b, sum_o = lax.psum((grad_w, grad_b, grad_o), 'path')  32.6 us
    ppermute x2, starting transfers between devices, from_behind(): return lax.ppermute(shard, axis, pairs)  6.35 us
    ppermute x2, waiting for transfers between devices, from_behind(): return lax.ppermute(shard, axis, pairs)  5.9 us
    dot_general x4, matrix products, net_parts(): delta = vol_curve[:, None] * jnp.dot(weight.T, slope, precision=hp)  5.69 us
    dot_general x3, matrix products, net_parts(): jnp.dot(weight, start_state, precision=hp) + bias[:, None]  5.56 us
    dot_general x4, matrix products, net_parts(): jnp.dot(weight, next_state, precision=hp) + bias[:, None]  4.56 us
  transfers between devices with their start and end apart: 3, of which 3 were waited for; matrix products, arithmetic and copies ran while one was open for 1% of the time, Pallas kernels for 0%

commit v1 on v0

v1 whole, which is shorter than its diff:
```python
import functools
import jax
import jax.numpy as jnp
from jax import lax
from jax.experimental import pallas as pl
from jax.experimental.pallas import tpu as pltpu
from jax.sharding import PartitionSpec as P

step_dt = 0.25
root_dt = 0.5
growth_factor = 1.0075
fund_spread = 0.5
norm_eps = 1e-06

f32 = jnp.float32
bf16 = jnp.bfloat16
LANES = 128
MESH = pl.DeviceIdType.MESH


def split(a):
    hi = a.astype(bf16)
    return hi, (a - hi.astype(f32)).astype(bf16)


def dot(a, b):
    return jnp.dot(a, b, preferred_element_type=f32)


def fold(a):
    return a[:, :LANES] + a[:, LANES:]


def wide(a, width):
    return jnp.concatenate([a] * (width // LANES), axis=1)


def kernel(
    n_path,
    reduce,
    start_ref,
    shock_ref,
    drift_ref,
    vol_ref,
    w_ref,
    bias_ref,
    outer_ref,
    date_ref,
    set_ref,
    given_ref,
    res_ref,
    *rest,
):
    if reduce:
        step_w_ref, step_b_ref, step_o_ref, curve_ref = rest[:4]
        rest = rest[4:]
    else:
        grad_ref, part_ref = rest[:2]
        rest = rest[2:]
    (
        x0,
        x1,
        sh,
        wp,
        wcat,
        wt,
        ocol,
        xcat,
        bt,
        h0s,
        h1s,
        s_hi,
        s_lo,
        dsum,
        x1sum,
        grad,
        swap_out,
        swap_in,
        swap_send,
        swap_recv,
        *rest,
    ) = rest
    feats, paths = start_ref.shape
    hidden = w_ref.shape[1]
    grp = lax.axis_index("grp")
    here = lax.axis_index("path")
    core = lax.rem(here, 2)
    chip = lax.div(here, 2)
    peers = n_path // 2
    half = hidden // 2
    other_grp = (1 - grp, here)
    other_core = (grp, chip * 2 + 1 - core)

    def peer(k):
        return lax.rem(chip + k, peers)

    barrier = pltpu.get_barrier_semaphore()
    pl.semaphore_signal(barrier, inc=1, device_id=other_grp, device_id_type=MESH)
    if reduce:
        pl.semaphore_signal(barrier, inc=1, device_id=other_core, device_id_type=MESH)
        for k in range(1, peers):
            pl.semaphore_signal(barrier, inc=1, device_id=(grp, peer(k) * 2 + core), device_id_type=MESH)

    rows = lax.broadcasted_iota(jnp.int32, (LANES, paths), 0)
    x0[...] = jnp.where(rows == feats, f32(1.0), f32(0.0))
    x0[0:feats, :] = start_ref[...]
    sh[...] = jnp.zeros_like(sh)
    sh[0:feats, :] = shock_ref[...]
    square = lax.broadcasted_iota(jnp.int32, (LANES, LANES), 0)
    curve_in = jnp.zeros((LANES, LANES), f32)
    pad = jnp.zeros((1, LANES - feats), f32)
    curve_in = jnp.where(square == 0, jnp.concatenate([drift_ref[...], pad], axis=1), curve_in)
    curve_in = jnp.where(square == 1, jnp.concatenate([vol_ref[...], pad], axis=1), curve_in)
    curve_col = curve_in.T
    drift = curve_col[:, 0:1]
    vol = curve_col[:, 1:2]
    shocks = sh[...]
    now = x0[...]
    nxt = now + drift * step_dt + vol * root_dt * shocks
    x1[...] = nxt
    for i, a in enumerate((now, nxt)):
        hi, lo = split(a)
        cols = slice(i * paths, (i + 1) * paths)
        xcat[0:LANES, cols] = hi
        xcat[LANES : 2 * LANES, cols] = hi
        xcat[2 * LANES :, cols] = lo
    wp[...] = jnp.zeros_like(wp)
    wp[:, 0:feats] = w_ref[0]
    dsum[...] = jnp.zeros_like(dsum)
    x1sum[...] = jnp.zeros_like(x1sum)

    def forward(j, carry):
        v0, v1 = carry
        base = pl.multiple_of(j * 2 * LANES, 2 * LANES)
        for k in range(2):
            r = pl.ds(pl.multiple_of(base + k * LANES, LANES), LANES)
            extra = jnp.where(square == feats, bias_ref[:, r], f32(0.0))
            extra = jnp.where(square == feats + 1, outer_ref[:, r], extra)
            w = wp[r, :]
            hi, lo = split(w.T)
            wt[0:LANES, r] = hi
            wt[LANES:, r] = lo
            extra = extra.T
            ocol[r, :] = jnp.broadcast_to(extra[:, feats + 1 : feats + 2], (LANES, LANES))
            hi, lo = split(w + extra)
            wcat[r, 0:LANES] = hi
            wcat[r, LANES : 2 * LANES] = lo
            wcat[r, 2 * LANES :] = hi
        r = pl.ds(base, 2 * LANES)
        z = dot(wcat[r, :], xcat[...])
        h0 = jnp.tanh(z[:, :paths])
        h1 = jnp.tanh(z[:, paths:])
        o = wide(ocol[r, :], paths)
        h0s[r, :] = h0
        h1s[r, :] = h1
        hi, lo = split(o * (1.0 - h0 * h0))
        s_hi[r, :] = hi
        s_lo[r, :] = lo
        d = dot(wt[:, r], hi)
        dsum[...] += d[:LANES] + d[LANES:] + dot(wt[0:LANES, r], lo)
        v0 = v0 + jnp.sum(o * h0, axis=0, keepdims=True)
        v1 = v1 + jnp.sum(o * h1, axis=0, keepdims=True)
        return v0, v1

    zero = jnp.zeros((1, paths), f32)
    v0, v1 = lax.fori_loop(0, hidden // (2 * LANES), forward, (zero, zero))
    inner = dsum[...]
    delta = vol * inner
    rest_own = -growth_factor * v0 - root_dt * jnp.sum(delta * shocks, axis=0, keepdims=True)
    square_own = jnp.sum(delta * delta, axis=0, keepdims=True)
    swap_out[0:1, :] = v1
    swap_out[1:2, :] = rest_own
    swap_out[2:3, :] = square_own
    swap_out[3:, :] = jnp.zeros((5, paths), f32)

    pl.semaphore_wait(barrier, peers + 1 if reduce else 1)
    swap = pltpu.make_async_remote_copy(
        src_ref=swap_out,
        dst_ref=swap_in,
        send_sem=swap_send.at[0],
        recv_sem=swap_recv.at[0],
        device_id=other_grp,
        device_id_type=MESH,
    )
    swap.start()
    for i, a in ((1, x0), (2, x1)):
        hi, lo = split(a[...].T)
        r = slice(i * paths, (i + 1) * paths)
        bt[r, 0:LANES] = hi
        bt[r, LANES:] = lo
    loss_row = zero
    for s in range(given_ref.shape[0]):
        loss_row = jnp.where(set_ref[...] == s, given_ref[s], loss_row)
    defaulted = date_ref[...] == 1
    clean = jnp.full((1, paths), grp, jnp.int32) == 0
    swap.wait()

    got_v1, got_rest, got_square = swap_in[0:1, :], swap_in[1:2, :], swap_in[2:3, :]
    clean_v1 = jnp.where(clean, v1, got_v1)
    res_clean = clean_v1 + jnp.where(clean, rest_own, got_rest)
    margin = jnp.sqrt(jnp.where(clean, square_own, got_square) + norm_eps)
    tail = jnp.exp(-jnp.abs(clean_v1))
    softplus = jnp.maximum(clean_v1, 0.0) + jnp.log1p(tail)
    sigmoid = jnp.where(clean_v1 >= 0.0, f32(1.0), tail) / (1.0 + tail)
    target = jnp.where(defaulted, loss_row * softplus, jnp.where(clean, got_v1, v1))
    res_xva = target + jnp.where(clean, got_rest, rest_own) + step_dt * fund_spread * margin
    residual = jnp.where(clean, res_clean, res_xva)
    res_ref[...] = residual
    per = f32(1.0 / (n_path * paths))
    weighted = residual * per
    weighted_xva = res_xva * per
    cot_now = -growth_factor * weighted
    cot_next = jnp.where(
        clean,
        weighted + jnp.where(defaulted, loss_row * sigmoid * weighted_xva, f32(0.0)),
        jnp.where(defaulted, f32(0.0), weighted),
    )
    pull = jnp.where(clean, step_dt * fund_spread * weighted_xva / margin, f32(0.0))
    cot_delta = -root_dt * weighted * shocks + pull * delta
    cot_inner = vol * cot_delta
    hi, lo = split(cot_inner)
    xcat[0:LANES, 0:paths] = hi
    xcat[LANES : 2 * LANES, 0:paths] = hi
    xcat[2 * LANES :, 0:paths] = lo
    hi, lo = split(cot_inner.T)
    bt[0:paths, 0:LANES] = hi
    bt[0:paths, LANES:] = lo
    lane = lax.broadcasted_iota(jnp.int32, (LANES, LANES), 1)

    def backward(base):
        r = pl.ds(pl.multiple_of(base, LANES), LANES)
        h0 = h0s[r, :]
        h1 = h1s[r, :]
        o = wide(ocol[r, :], paths)
        gap = 1.0 - h0 * h0
        t = dot(wcat[r, :], xcat[:, 0:paths])
        total = jnp.sum(t * gap + cot_now * h0 + cot_next * h1, axis=1, keepdims=True)
        y0_hi, y0_lo = split(o * gap * (cot_now - 2.0 * h0 * t))
        y1_hi, y1_lo = split(o * (1.0 - h1 * h1) * cot_next)
        a_hi = jnp.concatenate([s_hi[r, :], y0_hi, y1_hi], axis=1)
        a_lo = jnp.concatenate([s_lo[r, :], y0_lo, y1_lo], axis=1)
        g = fold(dot(a_hi, bt[...])) + dot(a_lo, bt[:, 0:LANES])
        grad[r, :] = g + jnp.where(lane == feats + 1, total, f32(0.0))
        back = dot(wt[:, r], y1_hi)
        x1sum[...] += back[:LANES] + back[LANES:] + dot(wt[0:LANES, r], y1_lo)

    def curve_rows():
        back = x1sum[...]
        by_drift = fold(step_dt * back).T
        by_vol = fold(root_dt * shocks * back + cot_delta * inner).T
        sub = lax.broadcasted_iota(jnp.int32, (8, LANES), 0)
        return jnp.where(
            sub == 0,
            jnp.sum(by_drift, axis=0, keepdims=True),
            jnp.where(sub == 1, jnp.sum(by_vol, axis=0, keepdims=True), f32(0.0)),
        )

    if not reduce:

        def whole_block(j, carry):
            backward(j * LANES)
            return carry

        lax.fori_loop(0, hidden // LANES, whole_block, 0)
        grad_ref[...] = grad[...]
        part_ref[...] = curve_rows()
        return

    (
        pair_in,
        peer_in,
        final,
        curve_out,
        curve_pair,
        curve_sum,
        curve_peer,
        curve_half,
        curve_far,
        pair_send,
        pair_recv,
        peer_send,
        peer_recv,
        all_send,
        all_recv,
        fwd_send,
        fwd_recv,
        curve_send,
        curve_recv,
        cpeer_send,
        cpeer_recv,
    ) = rest
    blocks = half // LANES
    chunk = half // peers
    per_block = LANES // chunk
    mine = core * half
    theirs = (1 - core) * half

    def turned(j):
        return lax.rem(j + 1 + lax.div(chip, per_block), blocks)

    def pair_copy(j):
        return pltpu.make_async_remote_copy(
            src_ref=grad.at[pl.ds(pl.multiple_of(theirs + j * LANES, LANES), LANES), :],
            dst_ref=pair_in.at[pl.ds(pl.multiple_of(j * LANES, LANES), LANES), :],
            send_sem=pair_send.at[j],
            recv_sem=pair_recv.at[j],
            device_id=other_core,
            device_id_type=MESH,
        )

    def chunk_rows(start, owner):
        return pl.ds(pl.multiple_of(start + owner * chunk, chunk), chunk)

    def peer_copy(owner, slot):
        return pltpu.make_async_remote_copy(
            src_ref=grad.at[chunk_rows(mine, owner), :],
            dst_ref=peer_in.at[slot],
            send_sem=peer_send.at[owner],
            recv_sem=peer_recv.at[slot],
            device_id=(grp, owner * 2 + core),
            device_id_type=MESH,
        )

    def all_copy(to, owner):
        return pltpu.make_async_remote_copy(
            src_ref=final.at[chunk_rows(mine, owner), :],
            dst_ref=final.at[chunk_rows(mine, owner), :],
            send_sem=all_send.at[to],
            recv_sem=all_recv.at[owner],
            device_id=(grp, to * 2 + core),
            device_id_type=MESH,
        )

    def fwd_copy(start, owner):
        return pltpu.make_async_remote_copy(
            src_ref=final.at[chunk_rows(start, owner), :],
            dst_ref=final.at[chunk_rows(start, owner), :],
            send_sem=fwd_send.at[owner],
            recv_sem=fwd_recv.at[owner],
            device_id=other_core,
            device_id_type=MESH,
        )

    def curve_copy(i, src, dst, to):
        return pltpu.make_async_remote_copy(
            src_ref=src,
            dst_ref=dst,
            send_sem=curve_send.at[i],
            recv_sem=curve_recv.at[i],
            device_id=to,
            device_id_type=MESH,
        )

    def cpeer_copy(to, slot):
        return pltpu.make_async_remote_copy(
            src_ref=curve_sum,
            dst_ref=curve_peer.at[slot],
            send_sem=cpeer_send.at[to],
            recv_sem=cpeer_recv.at[slot],
            device_id=(grp, to * 2 + core),
            device_id_type=MESH,
        )

    def their_block(j, carry):
        b = turned(j)
        backward(theirs + b * LANES)
        pair_copy(b).start()
        return carry

    def my_block(j, carry):
        b = turned(j)
        backward(mine + b * LANES)
        pair_copy(b).wait_recv()
        r = pl.ds(pl.multiple_of(mine + b * LANES, LANES), LANES)
        grad[r, :] += pair_in[pl.ds(pl.multiple_of(b * LANES, LANES), LANES), :]
        for k in range(per_block):
            owner = b * per_block + k

            @pl.when(owner != chip)
            def _():
                peer_copy(owner, chip).start()

        return carry

    lax.fori_loop(0, blocks, their_block, 0)
    lax.fori_loop(0, blocks, my_block, 0)
    curve_out[...] = curve_rows()
    pair_curve = curve_copy(0, curve_out, curve_pair, other_core)
    pair_curve.start()
    total = grad[chunk_rows(mine, chip), :]
    for k in range(1, peers):
        p = peer(k)
        peer_copy(p, p).wait_recv()
        total = total + peer_in[p]
    final[chunk_rows(mine, chip), :] = total
    for k in range(1, peers):
        all_copy(peer(k), chip).start()
    fwd_copy(mine, chip).start()
    pair_curve.wait_recv()
    curve_sum[...] = curve_out[...] + curve_pair[...]
    for k in range(1, peers):
        cpeer_copy(peer(k), chip).start()
    for k in range(1, peers):
        p = peer(k)
        all_copy(p, p).wait_recv()
        fwd_copy(mine, p).start()
    for p in range(peers):

        @pl.when(p != chip)
        def _():
            cpeer_copy(p, p).wait_recv()

        @pl.when(p == chip)
        def _():
            curve_peer[p] = curve_sum[...]

    curve = curve_peer[0]
    for p in range(1, peers):
        curve = curve + curve_peer[p]
    curve_half[...] = curve
    far_curve = curve_copy(1, curve_half, curve_far, other_grp)
    far_curve.start()
    for k in range(peers):
        fwd_copy(theirs, peer(k)).wait_recv()

    summed = final[...]
    parts = jnp.sum(jnp.sum(summed * summed, axis=0, keepdims=True), axis=1, keepdims=True)
    inverse = 1.0 / jnp.sqrt(parts / (hidden * feats + 2 * hidden) + norm_eps)
    step_w_ref[0] = final[:, 0:feats] * inverse
    for j in range(hidden // LANES):
        flipped = final[j * LANES : (j + 1) * LANES, :].T * inverse
        step_b_ref[:, j * LANES : (j + 1) * LANES] = flipped[feats : feats + 1, :]
        step_o_ref[:, j * LANES : (j + 1) * LANES] = flipped[feats + 1 : feats + 2, :]
    far_curve.wait_recv()
    curve = (curve_half[...] + curve_far[...])[0:2, 0:feats]
    mean = jnp.sum(jnp.sum(curve * curve, axis=0, keepdims=True), axis=1, keepdims=True) / (2 * feats)
    curve_ref[...] = curve / jnp.sqrt(mean + norm_eps)

    far_curve.wait_send()
    pair_curve.wait_send()
    for j in range(blocks):
        pair_copy(j).wait_send()
    for k in range(1, peers):
        peer_copy(peer(k), chip).wait_send()
        all_copy(peer(k), chip).wait_send()
        cpeer_copy(peer(k), chip).wait_send()
    for k in range(peers):
        fwd_copy(mine, peer(k)).wait_send()


def body(
    n_path,
    start_state,
    shocks,
    drift_rate,
    vol_curve,
    weight_in,
    bias_in,
    weight_out,
    default_date,
    netting_set,
    loss_given,
):
    feats, paths = start_state.shape
    hidden = weight_in.shape[1]
    peers = n_path // 2
    half = hidden // 2
    reduce = n_path % 2 == 0 and peers > 1 and half % (8 * peers) == 0 and half // peers <= LANES
    wide_row = (LANES, paths)
    tile = (8, LANES)
    scratch = [
        pltpu.VMEM(wide_row, f32),
        pltpu.VMEM(wide_row, f32),
        pltpu.VMEM(wide_row, f32),
        pltpu.VMEM((hidden, LANES), f32),
        pltpu.VMEM((hidden, 3 * LANES), bf16),
        pltpu.VMEM((2 * LANES, hidden), bf16),
        pltpu.VMEM((hidden, LANES), f32),
        pltpu.VMEM((3 * LANES, 2 * paths), bf16),
        pltpu.VMEM((3 * paths, 2 * LANES), bf16),
        pltpu.VMEM((hidden, paths), f32),
        pltpu.VMEM((hidden, paths), f32),
        pltpu.VMEM((hidden, paths), bf16),
        pltpu.VMEM((hidden, paths), bf16),
        pltpu.VMEM(wide_row, f32),
        pltpu.VMEM(wide_row, f32),
        pltpu.VMEM((hidden, LANES), f32),
        pltpu.VMEM((8, paths), f32),
        pltpu.VMEM((8, paths), f32),
        pltpu.SemaphoreType.DMA((1,)),
        pltpu.SemaphoreType.DMA((1,)),
    ]
    outs = [jax.ShapeDtypeStruct((1, paths), f32)]
    if reduce:
        blocks = half // LANES
        scratch += [
            pltpu.VMEM((half, LANES), f32),
            pltpu.VMEM((peers, half // peers, LANES), f32),
            pltpu.VMEM((hidden, LANES), f32),
            pltpu.VMEM(tile, f32),
            pltpu.VMEM(tile, f32),
            pltpu.VMEM(tile, f32),
            pltpu.VMEM((peers,) + tile, f32),
            pltpu.VMEM(tile, f32),
            pltpu.VMEM(tile, f32),
        ]
        scratch += [pltpu.SemaphoreType.DMA((blocks,))] * 2
        scratch += [pltpu.SemaphoreType.DMA((peers,))] * 6
        scratch += [pltpu.SemaphoreType.DMA((2,))] * 2
        scratch += [pltpu.SemaphoreType.DMA((peers,))] * 2
        outs += [
            jax.ShapeDtypeStruct((1, hidden, feats), f32),
            jax.ShapeDtypeStruct((1, hidden), f32),
            jax.ShapeDtypeStruct((1, hidden), f32),
            jax.ShapeDtypeStruct((2, feats), f32),
        ]
    else:
        outs += [jax.ShapeDtypeStruct((hidden, LANES), f32), jax.ShapeDtypeStruct(tile, f32)]
    vmem = pl.BlockSpec(memory_space=pltpu.VMEM)
    results = pl.pallas_call(
        functools.partial(kernel, n_path, reduce),
        out_shape=outs,
        in_specs=[vmem] * 9 + [pl.BlockSpec(memory_space=pltpu.SMEM)],
        out_specs=[vmem] * len(outs),
        scratch_shapes=scratch,
        compiler_params=pltpu.CompilerParams(
            collective_id=0, has_side_effects=True, vmem_limit_bytes=40 * 1024 * 1024
        ),
        name="bsde_step",
    )(
        start_state,
        shocks,
        drift_rate[None, :],
        vol_curve[None, :],
        weight_in,
        bias_in,
        weight_out,
        default_date[None, :],
        netting_set[None, :],
        loss_given,
    )
    if reduce:
        return tuple(results)
    residual, grad, part = results
    grad = lax.psum(grad, "path")
    curve = lax.psum(part, ("grp", "path"))[:2, :feats]
    scale = jnp.sqrt(jnp.sum(grad * grad) / (hidden * feats + 2 * hidden) + norm_eps)
    step = grad / scale
    curve_step = curve / jnp.sqrt(jnp.mean(curve * curve) + norm_eps)
    return (residual, step[None, :, :feats], step[None, :, feats], step[None, :, feats + 1], curve_step)


def solution(mesh):
    return jax.shard_map(
        functools.partial(body, mesh.shape["path"]),
        mesh=mesh,
        in_specs=(
            P(None, "path"),
            P(None, "path"),
            P(),
            P(),
            P("grp", None, None),
            P("grp", None),
            P("grp", None),
            P("path"),
            P("path"),
            P(),
        ),
        out_specs=(P("grp", "path"), P("grp", None, None), P("grp", None), P("grp", None), P()),
        check_vma=False,
    )
```

time: 187 us -> 35.1 us (0.19)
  blocking collectives: 72.2 us -> 0 us
  waiting for transfers between devices: 61.8 us -> 0 us
  Pallas kernels: 0 us -> 29.4 us
  matrix products: 19.3 us -> 0 us
  between operations: 17 us -> 0.8 us
  starting transfers between devices: 6.39 us -> 0 us
  other arithmetic: 6.35 us -> 0 us
    psum x2 -> x0, blocking collectives: 72.2 us -> none  [the longest x1 39.6 us: body(): sum_drift, sum_vol = lax.psum((grad_drift, grad_vol), ('grp', 'path'))]
    psum x1 -> x0, waiting for transfers between devices: 55.9 us -> none  [body(): sum_w, sum_b, sum_o = lax.psum((grad_w, grad_b, grad_o), 'path')]
    pallas_call x0 -> x1, Pallas kernels: none -> 29.4 us  [body(): pl.pallas_call(functools.partial(kernel, n_path, reduce), out_shape=outs,...]
    dot_general x15 -> x0, matrix products: 19.3 us -> none  [the longest x4 5.69 us: net_parts(): delta = vol_curve[:, None] * jnp.dot(weight.T, slope, precision=hp)]
    ppermute x2 -> x0, starting transfers between devices: 6.35 us -> none  [from_behind(): return lax.ppermute(shard, axis, pairs)]
    ppermute x2 -> x0, waiting for transfers between devices: 5.9 us -> none  [from_behind(): return lax.ppermute(shard, axis, pairs)]
    reduce_sum x6 -> x0, other arithmetic: 3.72 us -> none  [the longest x1 1.79 us: body(): jnp.sum(sum_w * sum_w) + jnp.sum(sum_b * sum_b) + jnp.sum(sum_o * sum_o)]
  transfers between devices with their start and end apart: 3 -> 0, of which waited for: 3 -> 0; matrix products, arithmetic and copies ran while one was open for 1% -> 0% of each run, Pallas kernels for 0% -> 0%
where the time goes in v1:
time: 35.1 us; the launch traced here: 34.9 us
  Pallas kernels  29.4 us (84%)
  local copies, waits for them, and re-layouts  4.71 us (13%)
  between operations  0.8 us (2%)
    pallas_call x1, Pallas kernels, body(): pl.pallas_call(functools.partial(kernel, n_path, reduce), out_shape=outs,...  29.4 us
    unnamed x23, local copies, waits for them, and re-layouts  3.69 us
    pallas_call x1, local copies, waits for them, and re-layouts, body(): pl.pallas_call(functools.partial(kernel, n_path, reduce), out_shape=outs,...  1.03 us

profile of v1, /device:TPU:0, one launch (start us, length us, event | category | flops | bytes accessed | tf_op | source)
XLA Modules:
  0.0 34.9 jit_solution(3713988134745952956)
XLA Ops:
  0.6 0.0 copy-start
  0.6 0.0 copy-start.1
  0.7 0.0 copy-start.2
  0.7 0.0 copy-start.3
  0.7 0.0 copy-start.4
  0.7 0.0 copy-start.5
  0.7 0.0 copy-start.6
  0.7 0.0 copy-start.7
  0.7 0.0 copy-start.8
  0.7 1.3 %copy.15.w_ref = f32[1,1024,100]{2,1,0:T(8,128)S(1)} copy(f32[1,1024,100]{1,0,2:T(1,128)} %param.14) | data formatting | bytes 819200 | tf_op args[4]
  2.1 0.0 copy-done
  2.1 0.0 copy-done.1
  2.1 0.0 copy-done.2
  2.1 0.0 copy-done.3
  2.1 0.0 copy-done.4
  2.1 0.0 copy-done.5
  2.1 0.0 copy-done.6
  2.1 0.0 copy-done.7
  2.2 29.4 %bsde_step.1 = (f32[1,256]{1,0:T(1,128)S(1)}, f32[1,1024,100]{2,1,0:T(8,128)S(1)}, f32[1,1024]{1,0:T(1,128)S(1)}, f32[1,1024]{1,0:T(1,128)S(1)}, f32[2,100]{1,0:T(2,128)S(1)}) custom-call(f32[100,256]{1,0:T(8,128)S(1)} %copy-done, f32[100,256]{1,0:T(8,128)S(1)} %copy-done.1, f32[1,100]{1,0:T(1,128)S(1)} %bitcast.6, f32[1,100]{1,0:T(1,128)S(1)} %bitcast.7, ...), custom_call_target="tpu_custom_call" | custom-call | tf_op jit(solution)/shard_map/bsde_step/pallas_call | solution.py:520
  31.6 1.0 %copy.16 = f32[1,1024,100]{1,0,2:T(1,128)} copy(f32[1,1024,100]{2,1,0:T(8,128)S(1)} %get-tuple-element.6) | data formatting | bytes 819200 | tf_op jit(solution)/shard_map/bsde_step/pallas_call | solution.py:520
  32.6 0.6 %copy.21 = f32[1,256]{1,0:T(1,128)} copy(f32[1,256]{1,0:T(1,128)S(1)} %get-tuple-element.15) | data formatting | bytes 2048
  33.2 0.6 %copy.22 = f32[1,1024]{1,0:T(1,128)} copy(f32[1,1024]{1,0:T(1,128)S(1)} %get-tuple-element.17) | data formatting | bytes 8192
  33.8 0.6 %copy.23 = f32[1,1024]{1,0:T(1,128)} copy(f32[1,1024]{1,0:T(1,128)S(1)} %get-tuple-element.18) | data formatting | bytes 8192
  34.4 0.6 %copy.24 = f32[2,100]{1,0:T(2,128)} copy(f32[2,100]{1,0:T(2,128)S(1)} %get-tuple-element.19) | data formatting | bytes 1600
  (1 shorter events, 0.0 us)
Async XLA Ops:
  0.6 1.4 %copy-start = (f32[100,256]{1,0:T(8,128)S(1)}, f32[100,256]{1,0:T(8,128)}, u32[]{:S(2)}) copy-start(f32[100,256]{1,0:T(8,128)} %start_ref.1) | copy-start | bytes 307204
  0.6 1.4 %copy-start.1 = (f32[100,256]{1,0:T(8,128)S(1)}, f32[100,256]{1,0:T(8,128)}, u32[]{:S(2)}) copy-start(f32[100,256]{1,0:T(8,128)} %shock_ref.1) | copy-start | bytes 307204
  0.7 1.4 %copy-start.2 = (f32[1,1024]{1,0:T(1,128)S(1)}, f32[1,1024]{1,0:T(1,128)}, u32[]{:S(2)}) copy-start(f32[1,1024]{1,0:T(1,128)} %bias_ref.1) | copy-start | bytes 12292
  0.7 1.4 %copy-start.3 = (f32[1,1024]{1,0:T(1,128)S(1)}, f32[1,1024]{1,0:T(1,128)}, u32[]{:S(2)}) copy-start(f32[1,1024]{1,0:T(1,128)} %outer_ref.1) | copy-start | bytes 12292
  0.7 1.4 %copy-start.4 = (s32[256]{0:T(256)S(1)}, s32[256]{0:T(256)}, u32[]{:S(2)}) copy-start(s32[256]{0:T(256)} %param.17) | copy-start | bytes 3076
  0.7 1.4 %copy-start.5 = (s32[256]{0:T(256)S(1)}, s32[256]{0:T(256)}, u32[]{:S(2)}) copy-start(s32[256]{0:T(256)} %param.18) | copy-start | bytes 3076
  0.7 1.4 %copy-start.6 = (f32[100]{0:T(128)S(1)}, f32[100]{0:T(128)}, u32[]{:S(2)}) copy-start(f32[100]{0:T(128)} %param.12) | copy-start | bytes 1204
  0.7 1.4 %copy-start.7 = (f32[100]{0:T(128)S(1)}, f32[100]{0:T(128)}, u32[]{:S(2)}) copy-start(f32[100]{0:T(128)} %param.13) | copy-start | bytes 1204
  0.7 1.4 %copy-start.8 = (f32[16]{0:T(128)S(1)}, f32[16]{0:T(128)}, u32[]{:S(2)}) copy-start(f32[16]{0:T(128)} %given_ref.1) | copy-start | bytes 196

commit v2 on v1

--- a/solution.py
+++ b/solution.py
@@ -51,12 +51,8 @@
     res_ref,
     *rest,
 ):
-    if reduce:
-        step_w_ref, step_b_ref, step_o_ref, curve_ref = rest[:4]
-        rest = rest[4:]
-    else:
-        grad_ref, part_ref = rest[:2]
-        rest = rest[2:]
+    sum_ref, curve_ref = rest[:2]
+    rest = rest[2:]
     (
         x0,
         x1,
@@ -81,7 +77,7 @@
         *rest,
     ) = rest
     feats, paths = start_ref.shape
-    hidden = w_ref.shape[1]
+    hidden = w_ref.shape[2]
     grp = lax.axis_index("grp")
     here = lax.axis_index("path")
     core = lax.rem(here, 2)
@@ -124,8 +120,11 @@
         xcat[0:LANES, cols] = hi
         xcat[LANES : 2 * LANES, cols] = hi
         xcat[2 * LANES :, cols] = lo
-    wp[...] = jnp.zeros_like(wp)
-    wp[:, 0:feats] = w_ref[0]
+    tail_row = feats // 8 * 8
+    wp[tail_row:, :] = jnp.zeros((LANES - tail_row, hidden), f32)
+    wp[0:feats, :] = w_ref[:, 0, :]
+    wp[feats : feats + 1, :] = bias_ref[...]
+    wp[feats + 1 : feats + 2, :] = outer_ref[...]
     dsum[...] = jnp.zeros_like(dsum)
     x1sum[...] = jnp.zeros_like(x1sum)
 
@@ -134,15 +133,13 @@
         base = pl.multiple_of(j * 2 * LANES, 2 * LANES)
         for k in range(2):
             r = pl.ds(pl.multiple_of(base + k * LANES, LANES), LANES)
-            extra = jnp.where(square == feats, bias_ref[:, r], f32(0.0))
-            extra = jnp.where(square == feats + 1, outer_ref[:, r], extra)
-            w = wp[r, :]
-            hi, lo = split(w.T)
+            w = wp[:, r]
+            hi, lo = split(w)
             wt[0:LANES, r] = hi
             wt[LANES:, r] = lo
-            extra = extra.T
-            ocol[r, :] = jnp.broadcast_to(extra[:, feats + 1 : feats + 2], (LANES, LANES))
-            hi, lo = split(w + extra)
+            w = w.T
+            ocol[r, :] = jnp.broadcast_to(w[:, feats + 1 : feats + 2], (LANES, LANES))
+            hi, lo = split(w)
             wcat[r, 0:LANES] = hi
             wcat[r, LANES : 2 * LANES] = lo
             wcat[r, 2 * LANES :] = hi
@@ -163,7 +160,7 @@
         return v0, v1
 
     zero = jnp.zeros((1, paths), f32)
-    v0, v1 = lax.fori_loop(0, hidden // (2 * LANES), forward, (zero, zero))
+    v0, v1 = lax.fori_loop(0, hidden // (2 * LANES), forward, (zero, zero), unroll=2)
     inner = dsum[...]
     delta = vol * inner
     rest_own = -growth_factor * v0 - root_dt * jnp.sum(delta * shocks, axis=0, keepdims=True)
@@ -225,10 +222,10 @@
     hi, lo = split(cot_inner.T)
     bt[0:paths, 0:LANES] = hi
     bt[0:paths, LANES:] = lo
-    lane = lax.broadcasted_iota(jnp.int32, (LANES, LANES), 1)
-
-    def backward(base):
-        r = pl.ds(pl.multiple_of(base, LANES), LANES)
+    lane = lax.broadcasted_iota(jnp.int32, (2 * LANES, LANES), 1)
+
+    def backward(b):
+        r = pl.ds(pl.multiple_of(b * LANES, 2 * LANES), 2 * LANES)
         h0 = h0s[r, :]
         h1 = h1s[r, :]
         o = wide(ocol[r, :], paths)
@@ -240,7 +237,10 @@
         a_hi = jnp.concatenate([s_hi[r, :], y0_hi, y1_hi], axis=1)
         a_lo = jnp.concatenate([s_lo[r, :], y0_lo, y1_lo], axis=1)
         g = fold(dot(a_hi, bt[...])) + dot(a_lo, bt[:, 0:LANES])
-        grad[r, :] = g + jnp.where(lane == feats + 1, total, f32(0.0))
+        g = g + jnp.where(lane == feats + 1, total, f32(0.0))
+        depth = grad.shape[1]
+        grad[b] = g[:LANES].T[:depth]
+        grad[b + 1] = g[LANES:].T[:depth]
         back = dot(wt[:, r], y1_hi)
         x1sum[...] += back[:LANES] + back[LANES:] + dot(wt[0:LANES, r], y1_lo)
 
@@ -258,17 +258,18 @@
     if not reduce:
 
         def whole_block(j, carry):
-            backward(j * LANES)
+            backward(j * 2)
             return carry
 
-        lax.fori_loop(0, hidden // LANES, whole_block, 0)
-        grad_ref[...] = grad[...]
-        part_ref[...] = curve_rows()
+        lax.fori_loop(0, hidden // (2 * LANES), whole_block, 0)
+        sum_ref[...] = grad[...]
+        curve_ref[...] = curve_rows()
         return
 
     (
         pair_in,
-        peer_in,
+        near_in,
+        far_in,
         final,
         curve_out,
         curve_pair,
@@ -278,68 +279,71 @@
         curve_far,
         pair_send,
         pair_recv,
-        peer_send,
-        peer_recv,
+        near_send,
+        near_recv,
+        far_send,
+        far_recv,
         all_send,
         all_recv,
         fwd_send,
         fwd_recv,
+        side_send,
+        side_recv,
         curve_send,
         curve_recv,
         cpeer_send,
         cpeer_recv,
     ) = rest
     blocks = half // LANES
-    chunk = half // peers
-    per_block = LANES // chunk
-    mine = core * half
-    theirs = (1 - core) * half
-
-    def turned(j):
-        return lax.rem(j + 1 + lax.div(chip, per_block), blocks)
-
-    def pair_copy(j):
+    own = blocks // 2
+    chips = peers // 2
+    per_block = chips // own
+    chunk = grad.shape[1] // per_block
+    side = lax.rem(chip, 2)
+    place = lax.div(chip, 2)
+    mine = core * blocks
+    theirs = (1 - core) * blocks
+    near = (grp, (place * 2 + 1 - side) * 2 + core)
+
+    def far(k):
+        return lax.rem(place + k, chips)
+
+    def part(start, on, owner):
+        return (
+            start + on * own + lax.div(owner, per_block),
+            pl.ds(pl.multiple_of(lax.rem(owner, per_block) * chunk, chunk), chunk),
+        )
+
+    def copy(src, dst, send, recv, to):
         return pltpu.make_async_remote_copy(
-            src_ref=grad.at[pl.ds(pl.multiple_of(theirs + j * LANES, LANES), LANES), :],
-            dst_ref=pair_in.at[pl.ds(pl.multiple_of(j * LANES, LANES), LANES), :],
-            send_sem=pair_send.at[j],
-            recv_sem=pair_recv.at[j],
-            device_id=other_core,
-            device_id_type=MESH,
+            src_ref=src, dst_ref=dst, send_sem=send, recv_sem=recv, device_id=to, device_id_type=MESH
         )
 
-    def chunk_rows(start, owner):
-        return pl.ds(pl.multiple_of(start + owner * chunk, chunk), chunk)
-
-    def peer_copy(owner, slot):
-        return pltpu.make_async_remote_copy(
-            src_ref=grad.at[chunk_rows(mine, owner), :],
-            dst_ref=peer_in.at[slot],
-            send_sem=peer_send.at[owner],
-            recv_sem=peer_recv.at[slot],
-            device_id=(grp, owner * 2 + core),
-            device_id_type=MESH,
-        )
+    def pair_copy(b):
+        return copy(grad.at[theirs + b], pair_in.at[b], pair_send.at[b], pair_recv.at[b], other_core)
+
+    def near_copy(i):
+        block = mine + (1 - side) * own + i
+        return copy(grad.at[block], near_in.at[i], near_send.at[i], near_recv.at[i], near)
+
+    def far_copy(owner, slot):
+        b, r = part(mine, side, owner)
+        to = (grp, (owner * 2 + side) * 2 + core)
+        return copy(grad.at[b, r], far_in.at[slot], far_send.at[owner], far_recv.at[slot], to)
 
     def all_copy(to, owner):
-        return pltpu.make_async_remote_copy(
-            src_ref=final.at[chunk_rows(mine, owner), :],
-            dst_ref=final.at[chunk_rows(mine, owner), :],
-            send_sem=all_send.at[to],
-            recv_sem=all_recv.at[owner],
-            device_id=(grp, to * 2 + core),
-            device_id_type=MESH,
-        )
-
-    def fwd_copy(start, owner):
-        return pltpu.make_async_remote_copy(
-            src_ref=final.at[chunk_rows(start, owner), :],
-            dst_ref=final.at[chunk_rows(start, owner), :],
-            send_sem=fwd_send.at[owner],
-            recv_sem=fwd_recv.at[owner],
-            device_id=other_core,
-            device_id_type=MESH,
-        )
+        b, r = part(mine, side, owner)
+        to_device = (grp, (to * 2 + side) * 2 + core)
+        return copy(final.at[b, r], final.at[b, r], all_send.at[to], all_recv.at[owner], to_device)
+
+    def side_copy(on, owner):
+        b, r = part(mine, on, owner)
+        return copy(final.at[b, r], final.at[b, r], side_send.at[owner], side_recv.at[owner], near)
+
+    def fwd_copy(start, on, owner):
+        b, r = part(start, on, owner)
+        i = on * chips + owner
+        return copy(final.at[b, r], final.at[b, r], fwd_send.at[i], fwd_recv.at[i], other_core)
 
     def curve_copy(i, src, dst, to):
         return pltpu.make_async_remote_copy(
@@ -361,49 +365,68 @@
             device_id_type=MESH,
         )
 
-    def their_block(j, carry):
-        b = turned(j)
-        backward(theirs + b * LANES)
+    def their_blocks(j, carry):
+        b = lax.rem((1 - side) * own + j * 2, blocks)
+        backward(theirs + b)
         pair_copy(b).start()
+        pair_copy(b + 1).start()
         return carry
 
-    def my_block(j, carry):
-        b = turned(j)
-        backward(mine + b * LANES)
-        pair_copy(b).wait_recv()
-        r = pl.ds(pl.multiple_of(mine + b * LANES, LANES), LANES)
-        grad[r, :] += pair_in[pl.ds(pl.multiple_of(b * LANES, LANES), LANES), :]
-        for k in range(per_block):
-            owner = b * per_block + k
-
-            @pl.when(owner != chip)
-            def _():
-                peer_copy(owner, chip).start()
-
+    def near_blocks(j, carry):
+        b = (1 - side) * own + j * 2
+        backward(mine + b)
+        for k in range(2):
+            pair_copy(b + k).wait_recv()
+            grad[mine + b + k] += pair_in[b + k]
+            near_copy(j * 2 + k).start()
         return carry
 
-    lax.fori_loop(0, blocks, their_block, 0)
-    lax.fori_loop(0, blocks, my_block, 0)
+    def my_blocks(j, carry):
+        b = side * own + j * 2
+        backward(mine + b)
+        for k in range(2):
+            pair_copy(b + k).wait_recv()
+            near_copy(j * 2 + k).wait_recv()
+            grad[mine + b + k] += pair_in[b + k] + near_in[j * 2 + k]
+            for i in range(per_block):
+                owner = (j * 2 + k) * per_block + i
+
+                @pl.when(owner != place)
+                def _():
+                    far_copy(owner, place).start()
+
+        return carry
+
+    lax.fori_loop(0, blocks // 2, their_blocks, 0)
+    lax.fori_loop(0, own // 2, near_blocks, 0)
+    lax.fori_loop(0, own // 2, my_blocks, 0)
     curve_out[...] = curve_rows()
     pair_curve = curve_copy(0, curve_out, curve_pair, other_core)
     pair_curve.start()
-    total = grad[chunk_rows(mine, chip), :]
-    for k in range(1, peers):
-        p = peer(k)
-        peer_copy(p, p).wait_recv()
-        total = total + peer_in[p]
-    final[chunk_rows(mine, chip), :] = total
-    for k in range(1, peers):
-        all_copy(peer(k), chip).start()
-    fwd_copy(mine, chip).start()
+    b, r = part(mine, side, place)
+    total = grad[b, r]
+    for k in range(1, chips):
+        p = far(k)
+        far_copy(p, p).wait_recv()
+        total = total + far_in[p]
+    final[b, r] = total
+    for k in range(1, chips):
+        all_copy(far(k), place).start()
+    side_copy(side, place).start()
+    fwd_copy(mine, side, place).start()
     pair_curve.wait_recv()
     curve_sum[...] = curve_out[...] + curve_pair[...]
     for k in range(1, peers):
         cpeer_copy(peer(k), chip).start()
-    for k in range(1, peers):
-        p = peer(k)
+    for k in range(1, chips):
+        p = far(k)
         all_copy(p, p).wait_recv()
-        fwd_copy(mine, p).start()
+        side_copy(side, p).start()
+        fwd_copy(mine, side, p).start()
+    for k in range(chips):
+        p = far(k)
+        side_copy(1 - side, p).wait_recv()
+        fwd_copy(mine, 1 - side, p).start()
     for p in range(peers):
 
         @pl.when(p != chip)
@@ -420,32 +443,47 @@
     curve_half[...] = curve
     far_curve = curve_copy(1, curve_half, curve_far, other_grp)
     far_curve.start()
-    for k in range(peers):
-        fwd_copy(theirs, peer(k)).wait_recv()
-
-    summed = final[...]
-    parts = jnp.sum(jnp.sum(summed * summed, axis=0, keepdims=True), axis=1, keepdims=True)
-    inverse = 1.0 / jnp.sqrt(parts / (hidden * feats + 2 * hidden) + norm_eps)
-    step_w_ref[0] = final[:, 0:feats] * inverse
-    for j in range(hidden // LANES):
-        flipped = final[j * LANES : (j + 1) * LANES, :].T * inverse
-        step_b_ref[:, j * LANES : (j + 1) * LANES] = flipped[feats : feats + 1, :]
-        step_o_ref[:, j * LANES : (j + 1) * LANES] = flipped[feats + 1 : feats + 2, :]
+    for on in (side, 1 - side):
+        for k in range(chips):
+            fwd_copy(theirs, on, far(k)).wait_recv()
+    sum_ref[...] = final[...]
     far_curve.wait_recv()
-    curve = (curve_half[...] + curve_far[...])[0:2, 0:feats]
-    mean = jnp.sum(jnp.sum(curve * curve, axis=0, keepdims=True), axis=1, keepdims=True) / (2 * feats)
-    curve_ref[...] = curve / jnp.sqrt(mean + norm_eps)
+    curve_ref[...] = curve_half[...] + curve_far[...]
 
     far_curve.wait_send()
     pair_curve.wait_send()
     for j in range(blocks):
         pair_copy(j).wait_send()
+    for j in range(own):
+        near_copy(j).wait_send()
+    for k in range(1, chips):
+        far_copy(far(k), place).wait_send()
+        all_copy(far(k), place).wait_send()
     for k in range(1, peers):
-        peer_copy(peer(k), chip).wait_send()
-        all_copy(peer(k), chip).wait_send()
         cpeer_copy(peer(k), chip).wait_send()
-    for k in range(peers):
-        fwd_copy(mine, peer(k)).wait_send()
+    for k in range(chips):
+        side_copy(side, far(k)).wait_send()
+        fwd_copy(mine, side, far(k)).wait_send()
+        fwd_copy(mine, 1 - side, far(k)).wait_send()
+
+
+def finish(res_ref, sum_ref, part_ref, res_out, step_w_ref, step_b_ref, step_o_ref, curve_ref):
+    feats, _, hidden = step_w_ref.shape
+    res_out[...] = res_ref[...]
+    squares = jnp.zeros(sum_ref.shape[1:], f32)
+    for j in range(hidden // LANES):
+        squares = squares + sum_ref[j] * sum_ref[j]
+    squares = jnp.sum(jnp.sum(squares, axis=0, keepdims=True), axis=1, keepdims=True)
+    inverse = 1.0 / jnp.sqrt(squares / (hidden * feats + 2 * hidden) + norm_eps)
+    for j in range(hidden // LANES):
+        r = slice(j * LANES, (j + 1) * LANES)
+        step = sum_ref[j] * inverse
+        step_w_ref[:, 0, r] = step[:feats]
+        step_b_ref[:, r] = step[feats : feats + 1]
+        step_o_ref[:, r] = step[feats + 1 : feats + 2]
+    curve = part_ref[0:2, 0:feats]
+    mean = jnp.sum(jnp.sum(curve * curve, axis=0, keepdims=True), axis=1, keepdims=True) / (2 * feats)
+    curve_ref[...] = curve / jnp.sqrt(mean + norm_eps)
 
 
 def body(
@@ -465,14 +503,20 @@
     hidden = weight_in.shape[1]
     peers = n_path // 2
     half = hidden // 2
-    reduce = n_path % 2 == 0 and peers > 1 and half % (8 * peers) == 0 and half // peers <= LANES
+    blocks = half // LANES
+    own = blocks // 2
+    chips = peers // 2
+    reduce = n_path % 4 == 0 and chips >= own and chips % own == 0 and chips // own <= 4
+    split_rows = 8 * (chips // own if reduce else 1)
+    depth = -(-(feats + 2) // split_rows) * split_rows
+    sums = (hidden // LANES, depth, LANES)
     wide_row = (LANES, paths)
     tile = (8, LANES)
     scratch = [
         pltpu.VMEM(wide_row, f32),
         pltpu.VMEM(wide_row, f32),
         pltpu.VMEM(wide_row, f32),
-        pltpu.VMEM((hidden, LANES), f32),
+        pltpu.VMEM((LANES, hidden), f32),
         pltpu.VMEM((hidden, 3 * LANES), bf16),
         pltpu.VMEM((2 * LANES, hidden), bf16),
         pltpu.VMEM((hidden, LANES), f32),
@@ -484,19 +528,23 @@
         pltpu.VMEM((hidden, paths), bf16),
         pltpu.VMEM(wide_row, f32),
         pltpu.VMEM(wide_row, f32),
-        pltpu.VMEM((hidden, LANES), f32),
+        pltpu.VMEM(sums, f32),
         pltpu.VMEM((8, paths), f32),
         pltpu.VMEM((8, paths), f32),
         pltpu.SemaphoreType.DMA((1,)),
         pltpu.SemaphoreType.DMA((1,)),
     ]
-    outs = [jax.ShapeDtypeStruct((1, paths), f32)]
+    outs = [
+        jax.ShapeDtypeStruct((1, paths), f32),
+        jax.ShapeDtypeStruct(sums, f32),
+        jax.ShapeDtypeStruct(tile, f32),
+    ]
     if reduce:
-        blocks = half // LANES
         scratch += [
-            pltpu.VMEM((half, LANES), f32),
-            pltpu.VMEM((peers, half // peers, LANES), f32),
-            pltpu.VMEM((hidden, LANES), f32),
+            pltpu.VMEM((blocks,) + sums[1:], f32),
+            pltpu.VMEM((own,) + sums[1:], f32),
+            pltpu.VMEM((chips, depth * own // chips, LANES), f32),
+            pltpu.VMEM(sums, f32),
             pltpu.VMEM(tile, f32),
             pltpu.VMEM(tile, f32),
             pltpu.VMEM(tile, f32),
@@ -505,19 +553,14 @@
             pltpu.VMEM(tile, f32),
         ]
         scratch += [pltpu.SemaphoreType.DMA((blocks,))] * 2
-        scratch += [pltpu.SemaphoreType.DMA((peers,))] * 6
+        scratch += [pltpu.SemaphoreType.DMA((own,))] * 2
+        scratch += [pltpu.SemaphoreType.DMA((chips,))] * 4
+        scratch += [pltpu.SemaphoreType.DMA((peers,))] * 2
+        scratch += [pltpu.SemaphoreType.DMA((chips,))] * 2
         scratch += [pltpu.SemaphoreType.DMA((2,))] * 2
         scratch += [pltpu.SemaphoreType.DMA((peers,))] * 2
-        outs += [
-            jax.ShapeDtypeStruct((1, hidden, feats), f32),
-            jax.ShapeDtypeStruct((1, hidden), f32),
-            jax.ShapeDtypeStruct((1, hidden), f32),
-            jax.ShapeDtypeStruct((2, feats), f32),
-        ]
-    else:
-        outs += [jax.ShapeDtypeStruct((hidden, LANES), f32), jax.ShapeDtypeStruct(tile, f32)]
     vmem = pl.BlockSpec(memory_space=pltpu.VMEM)
-    results = pl.pallas_call(
+    residual, total, curve = pl.pallas_call(
         functools.partial(kernel, n_path, reduce),
         out_shape=outs,
         in_specs=[vmem] * 9 + [pl.BlockSpec(memory_space=pltpu.SMEM)],
@@ -532,22 +575,31 @@
         shocks,
         drift_rate[None, :],
         vol_curve[None, :],
-        weight_in,
+        jnp.transpose(weight_in, (2, 0, 1)),
         bias_in,
         weight_out,
         default_date[None, :],
         netting_set[None, :],
         loss_given,
     )
-    if reduce:
-        return tuple(results)
-    residual, grad, part = results
-    grad = lax.psum(grad, "path")
-    curve = lax.psum(part, ("grp", "path"))[:2, :feats]
-    scale = jnp.sqrt(jnp.sum(grad * grad) / (hidden * feats + 2 * hidden) + norm_eps)
-    step = grad / scale
-    curve_step = curve / jnp.sqrt(jnp.mean(curve * curve) + norm_eps)
-    return (residual, step[None, :, :feats], step[None, :, feats], step[None, :, feats + 1], curve_step)
+    if not reduce:
+        total = lax.psum(total, "path")
+        curve = lax.psum(curve, ("grp", "path"))
+    residual, step_w, step_b, step_o, curve_step = pl.pallas_call(
+        finish,
+        out_shape=[
+            jax.ShapeDtypeStruct((1, paths), f32),
+            jax.ShapeDtypeStruct((feats, 1, hidden), f32),
+            jax.ShapeDtypeStruct((1, hidden), f32),
+            jax.ShapeDtypeStruct((1, hidden), f32),
+            jax.ShapeDtypeStruct((2, feats), f32),
+        ],
+        in_specs=[vmem] * 3,
+        out_specs=[vmem] * 5,
+        compiler_params=pltpu.CompilerParams(vmem_limit_bytes=16 * 1024 * 1024),
+        name="normalize",
+    )(residual, total, curve)
+    return (residual, jnp.transpose(step_w, (1, 2, 0)), step_b, step_o, curve_step)
 
 
 def solution(mesh):

time: 35.1 us -> 39.1 us (1.11)
  Pallas kernels: 29.4 us -> 32 us
  local copies, waits for them, and re-layouts: 4.71 us -> 6.12 us
    unnamed x23 -> x20, local copies, waits for them, and re-layouts: 3.69 us -> 6.12 us
    pallas_call x1, Pallas kernels: 29.4 us -> 30.9 us  [body(): pl.pallas_call(functools.partial(kernel, n_path, reduce), out_shape=outs,...]
    pallas_call x0 -> x1, Pallas kernels: none -> 1.13 us  [body(): pl.pallas_call(finish, out_shape=[jax.ShapeDtypeStruct((1, paths), f32),...]
    pallas_call x1 -> x0, local copies, waits for them, and re-layouts: 1.03 us -> none  [body(): pl.pallas_call(functools.partial(kernel, n_path, reduce), out_shape=outs,...]
where the time goes in v2:
time: 39.1 us; the launch traced here: 38.8 us
  Pallas kernels  32 us (82%)
  local copies, waits for them, and re-layouts  6.12 us (16%)
  between operations  0.68 us (2%)
    pallas_call x1, Pallas kernels, body(): pl.pallas_call(functools.partial(kernel, n_path, reduce), out_shape=outs,...  30.9 us
    unnamed x20, local copies, waits for them, and re-layouts  6.12 us
    pallas_call x1, Pallas kernels, body(): pl.pallas_call(finish, out_shape=[jax.ShapeDtypeStruct((1, paths), f32),...  1.13 us

profile of v2, /device:TPU:0, one launch (start us, length us, event | category | flops | bytes accessed | tf_op | source)
XLA Modules:
  0.0 38.8 jit_solution(15273348845125306468)
XLA Ops:
  0.6 0.0 copy-start.4
  0.6 0.0 copy-start.3
  0.7 0.0 copy-start.5
  0.7 0.7 %copy-done.4 = f32[1,1024]{1,0:T(1,128)S(1)} copy-done((f32[1,1024]{1,0:T(1,128)S(1)}, f32[1,1024]{1,0:T(1,128)}, u32[]{:S(2)}) %copy-start.4) | copy-done | bytes 4120
  1.3 0.0 copy-done.3
  1.3 0.0 copy-done.5
  1.3 0.0 copy-start
  1.3 1.0 %copy-done = f32[1,1024,100]{1,0,2:T(1,128)S(1)} copy-done((f32[1,1024,100]{1,0,2:T(1,128)S(1)}, f32[1,1024,100]{1,0,2:T(1,128)}, u32[]{:S(2)}) %copy-start) | copy-done | bytes 409624
  2.3 0.0 copy-start.1
  2.4 0.9 %copy-done.1 = f32[100,256]{1,0:T(8,128)S(1)} copy-done((f32[100,256]{1,0:T(8,128)S(1)}, f32[100,256]{1,0:T(8,128)}, u32[]{:S(2)}) %copy-start.1) | copy-done | bytes 102424
  3.2 0.0 copy-start.2
  3.2 0.9 %copy-done.2 = f32[100,256]{1,0:T(8,128)S(1)} copy-done((f32[100,256]{1,0:T(8,128)S(1)}, f32[100,256]{1,0:T(8,128)}, u32[]{:S(2)}) %copy-start.2) | copy-done | bytes 102424
  4.1 0.0 copy-start.6
  4.1 0.7 %copy-done.6 = s32[256]{0:T(256)S(1)} copy-done((s32[256]{0:T(256)S(1)}, s32[256]{0:T(256)}, u32[]{:S(2)}) %copy-start.6) | copy-done | bytes 1048
  4.8 0.0 copy-start.7
  4.8 0.7 %copy-done.7 = f32[100]{0:T(128)S(1)} copy-done((f32[100]{0:T(128)S(1)}, f32[100]{0:T(128)}, u32[]{:S(2)}) %copy-start.7) | copy-done | bytes 424
  5.5 0.0 copy-start.8
  5.5 0.7 %copy-done.8 = f32[100]{0:T(128)S(1)} copy-done((f32[100]{0:T(128)S(1)}, f32[100]{0:T(128)}, u32[]{:S(2)}) %copy-start.8) | copy-done | bytes 424
  6.1 0.0 copy-start.9
  6.1 0.7 %copy-done.9 = f32[16]{0:T(128)S(1)} copy-done((f32[16]{0:T(128)S(1)}, f32[16]{0:T(128)}, u32[]{:S(2)}) %copy-start.9) | copy-done | bytes 88
  6.8 30.9 %bsde_step.1 = (f32[1,256]{1,0:T(1,128)S(1)}, f32[8,112,128]{2,1,0:T(8,128)S(1)}, f32[8,128]{1,0:T(8,128)S(1)}) custom-call(f32[100,256]{1,0:T(8,128)S(1)} %copy-done.1, f32[100,256]{1,0:T(8,128)S(1)} %copy-done.2, f32[1,100]{1,0:T(1,128)S(1)} %bitcast.9, f32[1,100]{1,0:T(1,128)S(1)} %bitcast.10, f32[100,1,1024]{2,1,0:T(1,128)S(1)} %bitcast.6, ...), custom_call_target="tpu_custom_call" | custom-call | tf_op jit(solution)/shard_map/bsde_step/pallas_call | solution.py:563
  37.7 1.1 %normalize.1 = (f32[1,256]{1,0:T(1,128)}, f32[100,1,1024]{2,1,0:T(1,128)}, f32[1,1024]{1,0:T(1,128)}, f32[1,1024]{1,0:T(1,128)}, f32[2,100]{1,0:T(2,128)}) custom-call(f32[1,256]{1,0:T(1,128)S(1)} %get-tuple-element.13.res_ref, f32[8,112,128]{2,1,0:T(8,128)S(1)} %get-tuple-element.14.sum_ref, f32[8,128]{1,0:T(8,128)S(1)} %get-tuple-element.15.part_ref), custom_call_target="tpu_custom_call" | custom-call | tf_op jit(solution)/shard_map/normalize/pallas_call | solution.py:588
Async XLA Ops:
  0.6 0.7 %copy-start.4 = (f32[1,1024]{1,0:T(1,128)S(1)}, f32[1,1024]{1,0:T(1,128)}, u32[]{:S(2)}) copy-start(f32[1,1024]{1,0:T(1,128)} %outer_ref.1) | copy-start | bytes 12292
  0.6 0.7 %copy-start.3 = (f32[1,1024]{1,0:T(1,128)S(1)}, f32[1,1024]{1,0:T(1,128)}, u32[]{:S(2)}) copy-start(f32[1,1024]{1,0:T(1,128)} %bias_ref.1) | copy-start | bytes 12292
  0.7 0.7 %copy-start.5 = (s32[256]{0:T(256)S(1)}, s32[256]{0:T(256)}, u32[]{:S(2)}) copy-start(s32[256]{0:T(256)} %param.17) | copy-start | bytes 3076
  1.3 1.0 %copy-start = (f32[1,1024,100]{1,0,2:T(1,128)S(1)}, f32[1,1024,100]{1,0,2:T(1,128)}, u32[]{:S(2)}) copy-start(f32[1,1024,100]{1,0,2:T(1,128)} %param.14) | copy-start | bytes 1228804
  2.3 0.9 %copy-start.1 = (f32[100,256]{1,0:T(8,128)S(1)}, f32[100,256]{1,0:T(8,128)}, u32[]{:S(2)}) copy-start(f32[100,256]{1,0:T(8,128)} %start_ref.1) | copy-start | bytes 307204
  3.2 0.9 %copy-start.2 = (f32[100,256]{1,0:T(8,128)S(1)}, f32[100,256]{1,0:T(8,128)}, u32[]{:S(2)}) copy-start(f32[100,256]{1,0:T(8,128)} %shock_ref.1) | copy-start | bytes 307204
  4.1 0.7 %copy-start.6 = (s32[256]{0:T(256)S(1)}, s32[256]{0:T(256)}, u32[]{:S(2)}) copy-start(s32[256]{0:T(256)} %param.18) | copy-start | bytes 3076
  4.8 0.7 %copy-start.7 = (f32[100]{0:T(128)S(1)}, f32[100]{0:T(128)}, u32[]{:S(2)}) copy-start(f32[100]{0:T(128)} %param.12) | copy-start | bytes 1204
  5.5 0.7 %copy-start.8 = (f32[100]{0:T(128)S(1)}, f32[100]{0:T(128)}, u32[]{:S(2)}) copy-start(f32[100]{0:T(128)} %param.13) | copy-start | bytes 1204
  6.1 0.7 %copy-start.9 = (f32[16]{0:T(128)S(1)}, f32[16]{0:T(128)}, u32[]{:S(2)}) copy-start(f32[16]{0:T(128)} %given_ref.1) | copy-start | bytes 196

commit v3 on v2

--- a/solution.py
+++ b/solution.py
@@ -38,21 +38,12 @@
 def kernel(
     n_path,
     reduce,
-    start_ref,
-    shock_ref,
-    drift_ref,
-    vol_ref,
-    w_ref,
-    bias_ref,
-    outer_ref,
-    date_ref,
-    set_ref,
-    given_ref,
-    res_ref,
     *rest,
 ):
-    sum_ref, curve_ref = rest[:2]
-    rest = rest[2:]
+    inputs, rest = rest[:10], rest[10:]
+    res_ref, sum_ref, curve_ref = rest[:3]
+    local, load_sem, rest = rest[3:13], rest[13], rest[14:]
+    start_ref, shock_ref, drift_ref, vol_ref, w_ref, bias_ref, outer_ref, date_ref, set_ref, given_ref = local
     (
         x0,
         x1,
@@ -77,7 +68,7 @@
         *rest,
     ) = rest
     feats, paths = start_ref.shape
-    hidden = w_ref.shape[2]
+    hidden = w_ref.shape[1]
     grp = lax.axis_index("grp")
     here = lax.axis_index("path")
     core = lax.rem(here, 2)
@@ -90,12 +81,18 @@
     def peer(k):
         return lax.rem(chip + k, peers)
 
+    loads = [pltpu.make_async_copy(a.at[:, 0, :] if i == 4 else a, b, load_sem.at[i]) for i, (a, b) in enumerate(zip(inputs, local))]
+    for load in loads:
+        load.start()
     barrier = pltpu.get_barrier_semaphore()
     pl.semaphore_signal(barrier, inc=1, device_id=other_grp, device_id_type=MESH)
     if reduce:
         pl.semaphore_signal(barrier, inc=1, device_id=other_core, device_id_type=MESH)
         for k in range(1, peers):
             pl.semaphore_signal(barrier, inc=1, device_id=(grp, peer(k) * 2 + core), device_id_type=MESH)
+
+    for load in loads:
+        load.wait()
 
     rows = lax.broadcasted_iota(jnp.int32, (LANES, paths), 0)
     x0[...] = jnp.where(rows == feats, f32(1.0), f32(0.0))
@@ -122,7 +119,7 @@
         xcat[2 * LANES :, cols] = lo
     tail_row = feats // 8 * 8
     wp[tail_row:, :] = jnp.zeros((LANES - tail_row, hidden), f32)
-    wp[0:feats, :] = w_ref[:, 0, :]
+    wp[0:feats, :] = w_ref[...]
     wp[feats : feats + 1, :] = bias_ref[...]
     wp[feats + 1 : feats + 2, :] = outer_ref[...]
     dsum[...] = jnp.zeros_like(dsum)
@@ -186,8 +183,8 @@
         bt[r, 0:LANES] = hi
         bt[r, LANES:] = lo
     loss_row = zero
-    for s in range(given_ref.shape[0]):
-        loss_row = jnp.where(set_ref[...] == s, given_ref[s], loss_row)
+    for s in range(given_ref.shape[1]):
+        loss_row = jnp.where(set_ref[...] == s, given_ref[0:1, s : s + 1], loss_row)
     defaulted = date_ref[...] == 1
     clean = jnp.full((1, paths), grp, jnp.int32) == 0
     swap.wait()
@@ -512,7 +509,21 @@
     sums = (hidden // LANES, depth, LANES)
     wide_row = (LANES, paths)
     tile = (8, LANES)
-    scratch = [
+    inputs = [
+        start_state,
+        shocks,
+        drift_rate[None, :],
+        vol_curve[None, :],
+        jnp.transpose(weight_in, (2, 0, 1)),
+        bias_in,
+        weight_out,
+        default_date[None, :],
+        netting_set[None, :],
+        loss_given[None, :],
+    ]
+    scratch = [pltpu.VMEM((feats, hidden) if a.ndim == 3 else a.shape, a.dtype) for a in inputs]
+    scratch += [
+        pltpu.SemaphoreType.DMA((len(inputs),)),
         pltpu.VMEM(wide_row, f32),
         pltpu.VMEM(wide_row, f32),
         pltpu.VMEM(wide_row, f32),
@@ -563,25 +574,14 @@
     residual, total, curve = pl.pallas_call(
         functools.partial(kernel, n_path, reduce),
         out_shape=outs,
-        in_specs=[vmem] * 9 + [pl.BlockSpec(memory_space=pltpu.SMEM)],
+        in_specs=[pl.BlockSpec(memory_space=pltpu.HBM)] * len(inputs),
         out_specs=[vmem] * len(outs),
         scratch_shapes=scratch,
         compiler_params=pltpu.CompilerParams(
             collective_id=0, has_side_effects=True, vmem_limit_bytes=40 * 1024 * 1024
         ),
         name="bsde_step",
-    )(
-        start_state,
-        shocks,
-        drift_rate[None, :],
-        vol_curve[None, :],
-        jnp.transpose(weight_in, (2, 0, 1)),
-        bias_in,
-        weight_out,
-        default_date[None, :],
-        netting_set[None, :],
-        loss_given,
-    )
+    )(*inputs)
     if not reduce:
         total = lax.psum(total, "path")
         curve = lax.psum(curve, ("grp", "path"))

time: 39.1 us -> 37.2 us (0.951)
  local copies, waits for them, and re-layouts: 6.12 us -> 4.16 us
    unnamed x20, local copies, waits for them, and re-layouts: 6.12 us -> 4.16 us
where the time goes in v3:
time: 37.2 us; the launch traced here: 36.9 us
  Pallas kernels  32.1 us (86%)
  local copies, waits for them, and re-layouts  4.16 us (11%)
  between operations  0.7 us (2%)
    pallas_call x1, Pallas kernels, body(): pl.pallas_call(functools.partial(kernel, n_path, reduce), out_shape=outs,...  30.9 us
    unnamed x20, local copies, waits for them, and re-layouts  4.16 us
    pallas_call x1, Pallas kernels, body(): pl.pallas_call(finish, out_shape=[jax.ShapeDtypeStruct((1, paths), f32),...  1.13 us

profile of v3, /device:TPU:0, one launch (start us, length us, event | category | flops | bytes accessed | tf_op | source)
XLA Modules:
  0.0 36.9 jit_solution(5630351753735316793)
XLA Ops:
  0.6 0.0 copy-start.6
  0.6 0.0 copy-start.7
  0.7 0.0 copy-start.8
  0.7 0.0 copy-start.4
  0.7 0.0 copy-start.3
  0.7 0.0 copy-start.5
  0.7 0.6 %copy-done.6 = s32[256]{0:T(256)S(1)} copy-done((s32[256]{0:T(256)S(1)}, s32[256]{0:T(256)}, u32[]{:S(2)}) %copy-start.6) | copy-done | bytes 1048
  1.3 0.0 copy-done.7
  1.3 0.0 copy-done.8
  1.3 0.0 copy-done.4
  1.4 0.0 copy-done.3
  1.4 0.0 copy-done.5
  1.4 0.0 copy-start
  1.4 1.0 %copy-done = f32[1,1024,100]{1,0,2:T(1,128)S(1)} copy-done((f32[1,1024,100]{1,0,2:T(1,128)S(1)}, f32[1,1024,100]{1,0,2:T(1,128)}, u32[]{:S(2)}) %copy-start) | copy-done | bytes 409624
  2.4 0.0 copy-start.1
  2.4 0.9 %copy-done.1 = f32[100,256]{1,0:T(8,128)S(1)} copy-done((f32[100,256]{1,0:T(8,128)S(1)}, f32[100,256]{1,0:T(8,128)}, u32[]{:S(2)}) %copy-start.1) | copy-done | bytes 102424
  3.3 0.0 copy-start.2
  3.3 0.9 %copy-done.2 = f32[100,256]{1,0:T(8,128)S(1)} copy-done((f32[100,256]{1,0:T(8,128)S(1)}, f32[100,256]{1,0:T(8,128)}, u32[]{:S(2)}) %copy-start.2) | copy-done | bytes 102424
  4.2 0.0 copy-start.9
  4.2 0.7 %copy-done.9 = f32[16]{0:T(128)S(1)} copy-done((f32[16]{0:T(128)S(1)}, f32[16]{0:T(128)}, u32[]{:S(2)}) %copy-start.9) | copy-done | bytes 88
  4.8 30.9 %bsde_step.1 = (f32[1,256]{1,0:T(1,128)S(1)}, f32[8,112,128]{2,1,0:T(8,128)S(1)}, f32[8,128]{1,0:T(8,128)S(1)}) custom-call(f32[100,256]{1,0:T(8,128)S(1)} %copy-done.1, f32[100,256]{1,0:T(8,128)S(1)} %copy-done.2, f32[1,100]{1,0:T(1,128)S(1)} %bitcast.10, f32[1,100]{1,0:T(1,128)S(1)} %bitcast.11, f32[100,1,1024]{2,1,0:T(1,128)S(1)} %bitcast.7, ...), custom_call_target="tpu_custom_call" | custom-call | tf_op jit(solution)/shard_map/bsde_step/pallas_call | solution.py:574
  35.8 1.1 %normalize.1 = (f32[1,256]{1,0:T(1,128)}, f32[100,1,1024]{2,1,0:T(1,128)}, f32[1,1024]{1,0:T(1,128)}, f32[1,1024]{1,0:T(1,128)}, f32[2,100]{1,0:T(2,128)}) custom-call(f32[1,256]{1,0:T(1,128)S(1)} %get-tuple-element.13.res_ref, f32[8,112,128]{2,1,0:T(8,128)S(1)} %get-tuple-element.14.sum_ref, f32[8,128]{1,0:T(8,128)S(1)} %get-tuple-element.15.part_ref), custom_call_target="tpu_custom_call" | custom-call | tf_op jit(solution)/shard_map/normalize/pallas_call | solution.py:588
Async XLA Ops:
  0.6 0.7 %copy-start.6 = (s32[256]{0:T(256)S(1)}, s32[256]{0:T(256)}, u32[]{:S(2)}) copy-start(s32[256]{0:T(256)} %param.18) | copy-start | bytes 3076
  0.6 0.7 %copy-start.7 = (f32[100]{0:T(128)S(1)}, f32[100]{0:T(128)}, u32[]{:S(2)}) copy-start(f32[100]{0:T(128)} %param.12) | copy-start | bytes 1204
  0.7 0.7 %copy-start.8 = (f32[100]{0:T(128)S(1)}, f32[100]{0:T(128)}, u32[]{:S(2)}) copy-start(f32[100]{0:T(128)} %param.13) | copy-start | bytes 1204
  0.7 0.7 %copy-start.4 = (f32[1,1024]{1,0:T(1,128)S(1)}, f32[1,1024]{1,0:T(1,128)}, u32[]{:S(2)}) copy-start(f32[1,1024]{1,0:T(1,128)} %rest_6_.1) | copy-start | bytes 12292
  0.7 0.7 %copy-start.3 = (f32[1,1024]{1,0:T(1,128)S(1)}, f32[1,1024]{1,0:T(1,128)}, u32[]{:S(2)}) copy-start(f32[1,1024]{1,0:T(1,128)} %rest_5_.1) | copy-start | bytes 12292
  0.7 0.7 %copy-start.5 = (s32[256]{0:T(256)S(1)}, s32[256]{0:T(256)}, u32[]{:S(2)}) copy-start(s32[256]{0:T(256)} %param.17) | copy-start | bytes 3076
  1.4 1.0 %copy-start = (f32[1,1024,100]{1,0,2:T(1,128)S(1)}, f32[1,1024,100]{1,0,2:T(1,128)}, u32[]{:S(2)}) copy-start(f32[1,1024,100]{1,0,2:T(1,128)} %param.14) | copy-start | bytes 1228804
  2.4 0.9 %copy-start.1 = (f32[100,256]{1,0:T(8,128)S(1)}, f32[100,256]{1,0:T(8,128)}, u32[]{:S(2)}) copy-start(f32[100,256]{1,0:T(8,128)} %rest_0_.1) | copy-start | bytes 307204
  3.3 0.9 %copy-start.2 = (f32[100,256]{1,0:T(8,128)S(1)}, f32[100,256]{1,0:T(8,128)}, u32[]{:S(2)}) copy-start(f32[100,256]{1,0:T(8,128)} %rest_1_.1) | copy-start | bytes 307204
  4.2 0.7 %copy-start.9 = (f32[16]{0:T(128)S(1)}, f32[16]{0:T(128)}, u32[]{:S(2)}) copy-start(f32[16]{0:T(128)} %param.19) | copy-start | bytes 196

commit v4 on v3

--- a/solution.py
+++ b/solution.py
@@ -464,7 +464,19 @@
         fwd_copy(mine, 1 - side, far(k)).wait_send()
 
 
-def finish(res_ref, sum_ref, part_ref, res_out, step_w_ref, step_b_ref, step_o_ref, curve_ref):
+def finish(*refs):
+    inputs, (res_out, step_w_ref, step_b_ref, step_o_ref, curve_ref), local, load_sem = (
+        refs[:3],
+        refs[3:8],
+        refs[8:11],
+        refs[11],
+    )
+    loads = [pltpu.make_async_copy(a, b, load_sem.at[i]) for i, (a, b) in enumerate(zip(inputs, local))]
+    for load in loads:
+        load.start()
+    for load in loads:
+        load.wait()
+    res_ref, sum_ref, part_ref = local
     feats, _, hidden = step_w_ref.shape
     res_out[...] = res_ref[...]
     squares = jnp.zeros(sum_ref.shape[1:], f32)
@@ -578,7 +590,7 @@
         out_specs=[vmem] * len(outs),
         scratch_shapes=scratch,
         compiler_params=pltpu.CompilerParams(
-            collective_id=0, has_side_effects=True, vmem_limit_bytes=40 * 1024 * 1024
+            collective_id=0, has_side_effects=True, vmem_limit_bytes=60 * 1024 * 1024
         ),
         name="bsde_step",
     )(*inputs)
@@ -594,9 +606,11 @@
             jax.ShapeDtypeStruct((1, hidden), f32),
             jax.ShapeDtypeStruct((2, feats), f32),
         ],
-        in_specs=[vmem] * 3,
+        in_specs=[pl.BlockSpec(memory_space=pltpu.HBM)] * 3,
         out_specs=[vmem] * 5,
-        compiler_params=pltpu.CompilerParams(vmem_limit_bytes=16 * 1024 * 1024),
+        scratch_shapes=[pltpu.VMEM(a.shape, f32) for a in (residual, total, curve)]
+        + [pltpu.SemaphoreType.DMA((3,))],
+        compiler_params=pltpu.CompilerParams(vmem_limit_bytes=60 * 1024 * 1024),
         name="normalize",
     )(residual, total, curve)
     return (residual, jnp.transpose(step_w, (1, 2, 0)), step_b, step_o, curve_step)

time: 37.2 us -> 33.1 us (0.89)
  local copies, waits for them, and re-layouts: 4.16 us -> 0 us
    unnamed x20 -> x0, local copies, waits for them, and re-layouts: 4.16 us -> none
    pallas_call x1, Pallas kernels: 1.13 us -> 2.18 us  [body(): pl.pallas_call(finish, out_shape=[jax.ShapeDtypeStruct((1, paths), f32),...]
    pallas_call x1, Pallas kernels: 30.9 us -> 30.1 us  [body(): pl.pallas_call(functools.partial(kernel, n_path, reduce), out_shape=outs,...]
where the time goes in v4:
time: 33.1 us; the launch traced here: 32.9 us
  Pallas kernels  32.3 us (98%)
  between operations  0.64 us (2%)
    pallas_call x1, Pallas kernels, body(): pl.pallas_call(functools.partial(kernel, n_path, reduce), out_shape=outs,...  30.1 us
    pallas_call x1, Pallas kernels, body(): pl.pallas_call(finish, out_shape=[jax.ShapeDtypeStruct((1, paths), f32),...  2.18 us

profile of v4, /device:TPU:0, one launch (start us, length us, event | category | flops | bytes accessed | tf_op | source)
XLA Modules:
  0.0 32.9 jit_solution(12612568106944721231)
XLA Ops:
  0.6 30.1 %bsde_step.1 = (f32[1,256]{1,0:T(1,128)}, f32[8,112,128]{2,1,0:T(8,128)}, f32[8,128]{1,0:T(8,128)}) custom-call(f32[100,256]{1,0:T(8,128)} %rest_0_.1, f32[100,256]{1,0:T(8,128)} %rest_1_.1, f32[1,100]{1,0:T(1,128)} %bitcast.10, f32[1,100]{1,0:T(1,128)} %bitcast.11, f32[100,1,1024]{2,1,0:T(1,128)} %bitcast.7, f32[1,1024]{1,0:T(1,128)} %rest_5_.1, ...), custom_call_target="tpu_custom_call" | custom-call | tf_op jit(solution)/shard_map/bsde_step/pallas_call | solution.py:586
  30.7 2.2 %normalize.1 = (f32[1,256]{1,0:T(1,128)}, f32[100,1,1024]{2,1,0:T(1,128)}, f32[1,1024]{1,0:T(1,128)}, f32[1,1024]{1,0:T(1,128)}, f32[2,100]{1,0:T(2,128)}) custom-call(f32[1,256]{1,0:T(1,128)} %get-tuple-element.13.refs_0_, f32[8,112,128]{2,1,0:T(8,128)} %get-tuple-element.14.refs_1_, f32[8,128]{1,0:T(8,128)} %get-tuple-element.15.refs_2_), custom_call_target="tpu_custom_call" | custom-call | tf_op jit(solution)/shard_map/normalize/pallas_call | solution.py:600

commit v5 on v4

--- a/solution.py
+++ b/solution.py
@@ -42,7 +42,7 @@
 ):
     inputs, rest = rest[:10], rest[10:]
     res_ref, sum_ref, curve_ref = rest[:3]
-    local, load_sem, rest = rest[3:13], rest[13], rest[14:]
+    local, load_sem, save_sem, rest = rest[3:13], rest[13], rest[14], rest[15:]
     start_ref, shock_ref, drift_ref, vol_ref, w_ref, bias_ref, outer_ref, date_ref, set_ref, given_ref = local
     (
         x0,
@@ -91,7 +91,7 @@
         for k in range(1, peers):
             pl.semaphore_signal(barrier, inc=1, device_id=(grp, peer(k) * 2 + core), device_id_type=MESH)
 
-    for load in loads:
+    for load in loads[:4] + loads[5:]:
         load.wait()
 
     rows = lax.broadcasted_iota(jnp.int32, (LANES, paths), 0)
@@ -119,6 +119,7 @@
         xcat[2 * LANES :, cols] = lo
     tail_row = feats // 8 * 8
     wp[tail_row:, :] = jnp.zeros((LANES - tail_row, hidden), f32)
+    loads[4].wait()
     wp[0:feats, :] = w_ref[...]
     wp[feats : feats + 1, :] = bias_ref[...]
     wp[feats + 1 : feats + 2, :] = outer_ref[...]
@@ -157,7 +158,7 @@
         return v0, v1
 
     zero = jnp.zeros((1, paths), f32)
-    v0, v1 = lax.fori_loop(0, hidden // (2 * LANES), forward, (zero, zero), unroll=2)
+    v0, v1 = lax.fori_loop(0, hidden // (2 * LANES), forward, (zero, zero), unroll=4)
     inner = dsum[...]
     delta = vol * inner
     rest_own = -growth_factor * v0 - root_dt * jnp.sum(delta * shocks, axis=0, keepdims=True)
@@ -259,7 +260,9 @@
             return carry
 
         lax.fori_loop(0, hidden // (2 * LANES), whole_block, 0)
-        sum_ref[...] = grad[...]
+        save = pltpu.make_async_copy(grad, sum_ref, save_sem.at[0])
+        save.start()
+        save.wait()
         curve_ref[...] = curve_rows()
         return
 
@@ -440,13 +443,20 @@
     curve_half[...] = curve
     far_curve = curve_copy(1, curve_half, curve_far, other_grp)
     far_curve.start()
+    saves = [
+        pltpu.make_async_copy(final.at[pl.ds(h, blocks)], sum_ref.at[pl.ds(h, blocks)], save_sem.at[i])
+        for i, h in enumerate((mine, theirs))
+    ]
+    saves[0].start()
     for on in (side, 1 - side):
         for k in range(chips):
             fwd_copy(theirs, on, far(k)).wait_recv()
-    sum_ref[...] = final[...]
+    saves[1].start()
     far_curve.wait_recv()
     curve_ref[...] = curve_half[...] + curve_far[...]
 
+    for save in saves:
+        save.wait()
     far_curve.wait_send()
     pair_curve.wait_send()
     for j in range(blocks):
@@ -536,6 +546,7 @@
     scratch = [pltpu.VMEM((feats, hidden) if a.ndim == 3 else a.shape, a.dtype) for a in inputs]
     scratch += [
         pltpu.SemaphoreType.DMA((len(inputs),)),
+        pltpu.SemaphoreType.DMA((2,)),
         pltpu.VMEM(wide_row, f32),
         pltpu.VMEM(wide_row, f32),
         pltpu.VMEM(wide_row, f32),
@@ -587,7 +598,7 @@
         functools.partial(kernel, n_path, reduce),
         out_shape=outs,
         in_specs=[pl.BlockSpec(memory_space=pltpu.HBM)] * len(inputs),
-        out_specs=[vmem] * len(outs),
+        out_specs=[vmem, pl.BlockSpec(memory_space=pltpu.HBM), vmem],
         scratch_shapes=scratch,
         compiler_params=pltpu.CompilerParams(
             collective_id=0, has_side_effects=True, vmem_limit_bytes=60 * 1024 * 1024

time: 33.1 us -> 34 us (1.027)
  Pallas kernels: 32.3 us -> 33.2 us
    pallas_call x1, Pallas kernels: 30.1 us -> 31.1 us  [body(): pl.pallas_call(functools.partial(kernel, n_path, reduce), out_shape=outs,...]
where the time goes in v5:
time: 34 us; the launch traced here: 33.9 us
  Pallas kernels  33.2 us (98%)
  between operations  0.64 us (2%)
    pallas_call x1, Pallas kernels, body(): pl.pallas_call(functools.partial(kernel, n_path, reduce), out_shape=outs,...  31.1 us
    pallas_call x1, Pallas kernels, body(): pl.pallas_call(finish, out_shape=[jax.ShapeDtypeStruct((1, paths), f32),...  2.18 us

profile of v5, /device:TPU:0, one launch (start us, length us, event | category | flops | bytes accessed | tf_op | source)
XLA Modules:
  0.0 33.9 jit_solution(1335137004627287556)
XLA Ops:
  0.6 31.1 %bsde_step.1 = (f32[1,256]{1,0:T(1,128)}, f32[8,112,128]{2,1,0:T(8,128)}, f32[8,128]{1,0:T(8,128)}) custom-call(f32[100,256]{1,0:T(8,128)} %rest_0_.1, f32[100,256]{1,0:T(8,128)} %rest_1_.1, f32[1,100]{1,0:T(1,128)} %bitcast.10, f32[1,100]{1,0:T(1,128)} %bitcast.11, f32[100,1,1024]{2,1,0:T(1,128)} %bitcast.7, f32[1,1024]{1,0:T(1,128)} %rest_5_.1, ...), custom_call_target="tpu_custom_call" | custom-call | tf_op jit(solution)/shard_map/bsde_step/pallas_call | solution.py:597
  31.7 2.2 %normalize.1 = (f32[1,256]{1,0:T(1,128)}, f32[100,1,1024]{2,1,0:T(1,128)}, f32[1,1024]{1,0:T(1,128)}, f32[1,1024]{1,0:T(1,128)}, f32[2,100]{1,0:T(2,128)}) custom-call(f32[1,256]{1,0:T(1,128)} %get-tuple-element.13.refs_0_, f32[8,112,128]{2,1,0:T(8,128)} %get-tuple-element.14.refs_1_, f32[8,128]{1,0:T(8,128)} %get-tuple-element.15.refs_2_), custom_call_target="tpu_custom_call" | custom-call | tf_op jit(solution)/shard_map/normalize/pallas_call | solution.py:611

commit v6 on v5

--- a/solution.py
+++ b/solution.py
@@ -158,7 +158,7 @@
         return v0, v1
 
     zero = jnp.zeros((1, paths), f32)
-    v0, v1 = lax.fori_loop(0, hidden // (2 * LANES), forward, (zero, zero), unroll=4)
+    v0, v1 = lax.fori_loop(0, hidden // (2 * LANES), forward, (zero, zero))
     inner = dsum[...]
     delta = vol * inner
     rest_own = -growth_factor * v0 - root_dt * jnp.sum(delta * shocks, axis=0, keepdims=True)

time: 34 us -> 32.8 us (0.965)
  Pallas kernels: 33.2 us -> 32 us
    pallas_call x1, Pallas kernels: 31.1 us -> 29.8 us  [body(): pl.pallas_call(functools.partial(kernel, n_path, reduce), out_shape=outs,...]
where the time goes in v6:
time: 32.8 us; the launch traced here: 32.7 us
  Pallas kernels  32 us (98%)
  between operations  0.64 us (2%)
    pallas_call x1, Pallas kernels, body(): pl.pallas_call(functools.partial(kernel, n_path, reduce), out_shape=outs,...  29.8 us
    pallas_call x1, Pallas kernels, body(): pl.pallas_call(finish, out_shape=[jax.ShapeDtypeStruct((1, paths), f32),...  2.18 us

profile of v6, /device:TPU:0, one launch (start us, length us, event | category | flops | bytes accessed | tf_op | source)
XLA Modules:
  0.0 32.7 jit_solution(4329651094430587779)
XLA Ops:
  0.6 29.8 %bsde_step.1 = (f32[1,256]{1,0:T(1,128)}, f32[8,112,128]{2,1,0:T(8,128)}, f32[8,128]{1,0:T(8,128)}) custom-call(f32[100,256]{1,0:T(8,128)} %rest_0_.1, f32[100,256]{1,0:T(8,128)} %rest_1_.1, f32[1,100]{1,0:T(1,128)} %bitcast.10, f32[1,100]{1,0:T(1,128)} %bitcast.11, f32[100,1,1024]{2,1,0:T(1,128)} %bitcast.7, f32[1,1024]{1,0:T(1,128)} %rest_5_.1, ...), custom_call_target="tpu_custom_call" | custom-call | tf_op jit(solution)/shard_map/bsde_step/pallas_call | solution.py:597
  30.5 2.2 %normalize.1 = (f32[1,256]{1,0:T(1,128)}, f32[100,1,1024]{2,1,0:T(1,128)}, f32[1,1024]{1,0:T(1,128)}, f32[1,1024]{1,0:T(1,128)}, f32[2,100]{1,0:T(2,128)}) custom-call(f32[1,256]{1,0:T(1,128)} %get-tuple-element.13.refs_0_, f32[8,112,128]{2,1,0:T(8,128)} %get-tuple-element.14.refs_1_, f32[8,128]{1,0:T(8,128)} %get-tuple-element.15.refs_2_), custom_call_target="tpu_custom_call" | custom-call | tf_op jit(solution)/shard_map/normalize/pallas_call | solution.py:611
